TPU v7x, 32 devices: a whole 2x2x4 slice. The times are simulated.
32 devices in a mesh: client: 16 (over z, y, x), chan: 2 (over core).
Axes of the slice: x: 2, y: 2, z: 4, core: 2. Of those that a mesh axis runs over, the one named last changes fastest.
Arguments:
- features: bfloat16 [16, 3136, 2048], P('client', None, 'chan'), may hold values from -6 to 6
- labels: int32 [16, 64], P('client'), may hold values from 0 to 99
- mask: int32 [16], P('client'), may hold values 0 or 1
- base_master: float32 [32, 272, 512], P(('client', 'chan')), may hold values from -0.176776695 to 0.176776695, as said below
- base_momentum: float32 [32, 272, 512], P(('client', 'chan')), may hold values from -0.0234375 to 0.0234375
- global_base: float32 [32, 272, 512], P(('client', 'chan')), may hold values from -0.176776695 to 0.176776695, as said below
- norm_params: float32 [16, 2, 2, 1536], P('client', None, 'chan'), may hold values from -0.9 to 1.3, as said below
- norm_first: float32 [16, 2, 2, 1536], P('client', None, 'chan'), may hold values from -0.00061035156 to 0.00061035156
- norm_second: float32 [16, 2, 2, 1536], P('client', None, 'chan'), may hold values from 5.340576e-09 to 3.2043456e-08
- head: float32 [16, 2048, 100], P('client', 'chan'), may hold values from -0.25 to 0.25
- head_first: float32 [16, 2048, 100], P('client', 'chan'), may hold values from -0.015625 to 0.015625
- head_second: float32 [16, 2048, 100], P('client', 'chan'), may hold values from 4.6875e-06 to 1.5625e-05
Outputs:
- loss: float32 [2], replicated
- base_new: float32 [32, 272, 512], P(('client', 'chan'))
- base_momentum_new: float32 [32, 272, 512], P(('client', 'chan'))
- base_low: bfloat16 [32, 272, 512], P(('client', 'chan'))
- norm_new: float32 [16, 2, 2, 1536], P('client', None, 'chan')
- norm_first_new: float32 [16, 2, 2, 1536], P('client', None, 'chan')
- norm_second_new: float32 [16, 2, 2, 1536], P('client', None, 'chan')
- head_new: float32 [16, 2048, 100], P('client', 'chan')
- head_first_new: float32 [16, 2048, 100], P('client', 'chan')
- head_second_new: float32 [16, 2048, 100], P('client', 'chan')
Inputs may be any that keep to these rules, and one draw needn't show every extreme that they name: `base_master`: base weights with entries of about one over the root of each matrix's fan-in. `global_base`: drawn like base_master, independently. `norm_params`: gains near one, biases of both signs.
All inputs are finite; a program needn't handle non-finite values. No bound on the sum of `mask` on one device may be relied on, other than what follows from the above.
Results may differ from a plain program's by a relative error of at most 0.012.
Values may be sent and summed in bfloat16 or wider, within the bound.
A program may use at most 512 MiB of HBM per device.

v0:
```python
import jax
import jax.numpy as jnp
from jax import lax
from jax.sharding import PartitionSpec as P

NS_STEPS = 5
STEP = 10


precise = lax.Precision.HIGHEST
norm_epsilon = 1e-05
prox_weight = 0.05
momentum_decay = 0.95
muon_rate = 0.3
muon_decay = 0.1
schulz_first = 3.4445
schulz_second = -4.775
schulz_third = 2.0315
adam_first = 0.9
adam_second = 0.95
adam_epsilon = 1e-08
head_rate = 0.01
head_decay = 0.05
norm_rate = 0.5


def patches_of(hidden, images):
    width = hidden.shape[1]
    grid = jnp.pad(hidden.reshape(images, 7, 7, width), ((0, 0), (1, 1), (1, 1), (0, 0)))
    taps = [
        grid[:, shift_y : shift_y + 7, shift_x : shift_x + 7, :]
        for shift_y in range(3)
        for shift_x in range(3)
    ]
    return jnp.concatenate(taps, axis=-1).reshape(images * 49, 9 * width)


def fold_patches(grads, images, width):
    columns = grads.reshape(images, 7, 7, 9, width)
    total = jnp.zeros((images, 9, 9, width), jnp.float32)
    for shift_y in range(3):
        for shift_x in range(3):
            total = total + jnp.pad(
                columns[:, :, :, 3 * shift_y + shift_x, :],
                ((0, 0), (shift_y, 2 - shift_y), (shift_x, 2 - shift_x), (0, 0)),
            )
    return total[:, 1:8, 1:8, :].reshape(images * 49, width)


def norm_forward(act, gain, bias):
    centred = act - jnp.mean(act, axis=0)
    scale = lax.rsqrt(jnp.mean(centred * centred, axis=0) + norm_epsilon)
    normed = centred * scale
    return (normed * gain + bias, normed, scale)


def norm_backward(grad_out, normed, scale, gain):
    scaled = grad_out * gain
    grad_in = scale * (
        scaled - jnp.mean(scaled, axis=0) - normed * jnp.mean(scaled * normed, axis=0)
    )
    return (grad_in, jnp.sum(grad_out * normed, axis=0), jnp.sum(grad_out, axis=0))


def silu_slope(value):
    sigma = jax.nn.sigmoid(value)
    return sigma * (1.0 + value * (1.0 - sigma))


def contract_rows(left, right):
    return lax.dot_general(
        left, right, (((0,), (0,)), ((), ())), preferred_element_type=jnp.float32
    )


def contract_cols(left, right):
    return lax.dot_general(
        left, right, (((1,), (1,)), ((), ())), preferred_element_type=jnp.float32
    )


def gram_of(section):
    return lax.dot_general(section, section, (((0,), (0,)), ((), ())), precision=precise)


def gram_sum(first_part, middle_part, last_part):
    return lax.psum(
        (gram_of(first_part), gram_of(middle_part), gram_of(last_part)), ("client", "chan")
    )


def schulz_step(current, gram):
    product = jnp.dot(current, gram, precision=precise)
    return (
        schulz_first * current
        + schulz_second * product
        + schulz_third * jnp.dot(product, gram, precision=precise)
    )


def adam_update(param, grad, first, second, rate, decay):
    first = adam_first * first + (1.0 - adam_first) * grad
    second = adam_second * second + (1.0 - adam_second) * grad * grad
    first_hat = first / (1.0 - adam_first**STEP)
    second_hat = second / (1.0 - adam_second**STEP)
    return (
        param - rate * (first_hat / (jnp.sqrt(second_hat) + adam_epsilon) + decay * param),
        first,
        second,
    )


def on_device(
    features,
    labels,
    mask,
    base_master,
    base_momentum,
    global_base,
    norm_params,
    norm_first,
    norm_second,
    head,
    head_first,
    head_second,
):
    halves = lax.axis_size("chan")
    blocks = lax.axis_size("client") * halves
    local_x = features[0]
    pixels, feat_half = local_x.shape
    width = base_master.shape[2]
    channels = feat_half * halves
    images = labels.shape[1]
    rows_first = channels // blocks
    rows_mid = 9 * width // blocks
    middle_half = width // halves
    master = base_master[0]
    low_master = master.astype(jnp.bfloat16)
    first_piece, middle_piece, last_piece = (
        lax.all_to_all(low_master[:rows_first], "chan", split_axis=1, concat_axis=0, tiled=True),
        lax.all_to_all(
            low_master[rows_first : rows_first + rows_mid],
            "chan",
            split_axis=1,
            concat_axis=0,
            tiled=True,
        ),
        lax.all_to_all(
            low_master[rows_first + rows_mid :], "chan", split_axis=1, concat_axis=0, tiled=True
        ),
    )
    reduce_weight, middle_weight, expand_weight = (
        lax.all_gather(first_piece, "client", axis=0, tiled=True),
        lax.all_gather(middle_piece, "client", axis=0, tiled=True),
        lax.all_gather(last_piece, "client", axis=0, tiled=True),
    )
    params = norm_params[0, :, 0, :]
    gain_one, bias_one = (params[0, :middle_half], params[1, :middle_half])
    gain_two, bias_two = (params[0, middle_half:width], params[1, middle_half:width])
    gain_three, bias_three = (params[0, width:], params[1, width:])
    inputs_all = lax.all_gather(local_x, "chan", axis=1, tiled=True)
    act_one = jnp.dot(inputs_all, reduce_weight, preferred_element_type=jnp.float32)
    norm_one, normed_one, scale_one = norm_forward(act_one, gain_one, bias_one)
    hidden_one = jax.nn.silu(norm_one).astype(jnp.bfloat16)
    full_one = lax.all_gather(hidden_one, "chan", axis=1, tiled=True)
    patches = patches_of(full_one, images)
    act_two = jnp.dot(patches, middle_weight, preferred_element_type=jnp.float32)
    norm_two, normed_two, scale_two = norm_forward(act_two, gain_two, bias_two)
    hidden_two = jax.nn.silu(norm_two).astype(jnp.bfloat16)
    act_three = lax.psum_scatter(
        contract_cols(hidden_two, expand_weight).astype(jnp.bfloat16),
        "chan",
        scatter_dimension=1,
        tiled=True,
    ).astype(jnp.float32)
    norm_three, normed_three, scale_three = norm_forward(act_three, gain_three, bias_three)
    total = norm_three + local_x.astype(jnp.float32)
    output = jax.nn.silu(total)
    pooled = jnp.mean(output.reshape(images, 49, feat_half), axis=1).astype(jnp.bfloat16)
    head_low = head[0].astype(jnp.bfloat16)
    logits = lax.psum(jnp.dot(pooled, head_low, preferred_element_type=jnp.float32), "chan")
    onehot = (labels[0][:, None] == jnp.arange(logits.shape[1])[None, :]).astype(jnp.float32)
    each_loss = jax.nn.logsumexp(logits, axis=1) - jnp.sum(logits * onehot, axis=1)
    flag = mask[0].astype(jnp.float32)
    loss_sum, count = lax.psum((flag * jnp.sum(each_loss), flag * images), "client")
    loss = jnp.stack([loss_sum, count])
    grad_logits = (flag / images * (jax.nn.softmax(logits, axis=1) - onehot)).astype(jnp.bfloat16)
    grad_head = contract_rows(pooled, grad_logits)
    grad_pooled = contract_cols(grad_logits, head_low)
    grad_output = jnp.broadcast_to(grad_pooled[:, None, :] / 49.0, (images, 49, feat_half)).reshape(
        pixels, feat_half
    )
    grad_in_three, grad_gain_three, grad_bias_three = norm_backward(
        grad_output * silu_slope(total), normed_three, scale_three, gain_three
    )
    grad_act_three = grad_in_three.astype(jnp.bfloat16)
    grad_three_all = lax.all_gather(grad_act_three, "chan", axis=1, tiled=True)
    grad_hidden_two = jnp.dot(grad_three_all, expand_weight, preferred_element_type=jnp.float32)
    grad_expand = contract_rows(grad_three_all, hidden_two)
    grad_in_two, grad_gain_two, grad_bias_two = norm_backward(
        grad_hidden_two * silu_slope(norm_two), normed_two, scale_two, gain_two
    )
    grad_act_two = grad_in_two.astype(jnp.bfloat16)
    grad_middle = contract_rows(patches, grad_act_two)
    grad_full_one = fold_patches(contract_cols(grad_act_two, middle_weight), images, width)
    grad_hidden_one = lax.psum_scatter(
        grad_full_one.astype(jnp.bfloat16), "chan", scatter_dimension=1, tiled=True
    ).astype(jnp.float32)
    grad_in_one, grad_gain_one, grad_bias_one = norm_backward(
        grad_hidden_one * silu_slope(norm_one), normed_one, scale_one, gain_one
    )
    grad_reduce = contract_rows(inputs_all, grad_in_one.astype(jnp.bfloat16))
    sum_reduce, sum_middle, sum_expand = (
        lax.psum_scatter(grad_reduce, "client", scatter_dimension=0, tiled=True),
        lax.psum_scatter(grad_middle, "client", scatter_dimension=0, tiled=True),
        lax.psum_scatter(grad_expand, "client", scatter_dimension=0, tiled=True),
    )
    block_reduce, block_middle, block_expand = (
        lax.all_to_all(
            sum_reduce.astype(jnp.bfloat16), "chan", split_axis=0, concat_axis=1, tiled=True
        ).astype(sum_reduce.dtype),
        lax.all_to_all(
            sum_middle.astype(jnp.bfloat16), "chan", split_axis=0, concat_axis=1, tiled=True
        ).astype(sum_middle.dtype),
        lax.all_to_all(
            sum_expand.astype(jnp.bfloat16), "chan", split_axis=0, concat_axis=1, tiled=True
        ).astype(sum_expand.dtype),
    )
    grad_base = jnp.concatenate(
        [block_reduce, block_middle, block_expand], axis=0
    ) + prox_weight * (master - global_base[0])
    momentum_new = momentum_decay * base_momentum[0] + grad_base
    sections = [
        momentum_new[:rows_first],
        momentum_new[rows_first : rows_first + rows_mid],
        momentum_new[rows_first + rows_mid :],
    ]
    raw_grams = gram_sum(sections[0], sections[1], sections[2])
    factors = [1.0 / (jnp.sqrt(jnp.trace(raw_grams[slot])) + 1e-07) for slot in range(3)]
    current = [sections[slot] * factors[slot] for slot in range(3)]
    grams = [raw_grams[slot] * (factors[slot] * factors[slot]) for slot in range(3)]
    for turn in range(NS_STEPS):
        if turn > 0:
            grams = gram_sum(current[0], current[1], current[2])
        current = [schulz_step(current[slot], grams[slot]) for slot in range(3)]
    ratio = (channels / width) ** 0.5
    ortho = jnp.concatenate([current[0] * ratio, current[1] * 3.0, current[2] * ratio], axis=0)
    base_new = master - muon_rate * (ortho + muon_decay * master)
    grad_norm = jnp.stack(
        [
            jnp.concatenate([grad_gain_one, grad_gain_two, grad_gain_three]),
            jnp.concatenate([grad_bias_one, grad_bias_two, grad_bias_three]),
        ]
    )[None, :, None, :]
    norm_new, norm_first_new, norm_second_new = adam_update(
        norm_params, grad_norm, norm_first, norm_second, norm_rate, 0.0
    )
    head_new, head_first_new, head_second_new = adam_update(
        head, grad_head[None], head_first, head_second, head_rate, head_decay
    )
    return (
        loss,
        base_new[None],
        momentum_new[None],
        base_new.astype(jnp.bfloat16)[None],
        norm_new,
        norm_first_new,
        norm_second_new,
        head_new,
        head_first_new,
        head_second_new,
    )


def solution(mesh):
    return jax.shard_map(
        on_device,
        mesh=mesh,
        in_specs=(
            P("client", None, "chan"),
            P("client", None),
            P("client"),
            P(("client", "chan"), None, None),
            P(("client", "chan"), None, None),
            P(("client", "chan"), None, None),
            P("client", None, "chan", None),
            P("client", None, "chan", None),
            P("client", None, "chan", None),
            P("client", "chan", None),
            P("client", "chan", None),
            P("client", "chan", None),
        ),
        out_specs=(
            P(),
            P(("client", "chan"), None, None),
            P(("client", "chan"), None, None),
            P(("client", "chan"), None, None),
            P("client", None, "chan", None),
            P("client", None, "chan", None),
            P("client", None, "chan", None),
            P("client", "chan", None),
            P("client", "chan", None),
            P("client", "chan", None),
        ),
        check_vma=False,
    )
```

profile of v0, /device:TPU:0, one launch (start us, length us, event | category | flops | bytes accessed | tf_op | source)
XLA Modules:
  0.0 1809.2 jit_solution(4132946813193475161)
XLA Ops:
  13.8 57.2 %all-gather.8.cloned.1.call-done = bf16[2048,256]{1,0:T(8,128)(2,1)} async-done(((bf16[128,256]{1,0:T(8,128)(2,1)}), bf16[2048,256]{1,0:T(8,128)(2,1)}) %all-gather.8.cloned.1.call-update) | async-done | bytes 1048592 | tf_op jit(solution)/shard_map/all_gather | solution.py:153
  71.0 25.6 %all-gather.18.cloned.1.call-done = bf16[1,3136,2048]{2,1,0:T(8,128)(2,1)} async-done(((bf16[1,3136,1024]{2,1,0:T(8,128)(2,1)}), bf16[1,3136,2048]{2,1,0:T(8,128)(2,1)}) %all-gather.18.cloned.1.call-update) | async-done | bytes 12845072 | tf_op jit(solution)/shard_map/all_gather | solution.py:161
  96.6 6.9 fusion.97
  107.5 4.6 all_to_all.97
  112.2 4.5 all_to_all.98
  120.5 6.1 reshape.265
  126.5 21.2 %pad_slice_fusion = (bf16[64,7,7,512]{3,2,1,0:T(8,128)(2,1)}, bf16[64,7,7,512]{3,2,1,0:T(8,128)(2,1)}, bf16[64,7,7,512]{3,2,1,0:T(8,128)(2,1)}, bf16[64,7,7,512]...) fusion(bf16[64,7,7,512]{3,2,1,0:T(8,128)(2,1)} %reshape.265), kind=kLoop, calls=%fused_computation | loop fusion | bytes 28901376 | tf_op jit(solution)/shard_map/slice | solution.py:31
  147.8 4.9 concatenate.69
  154.6 6.1 concatenate.70
  160.7 6.1 concatenate.71
  166.8 6.1 concatenate.72
  173.0 6.1 concatenate.73
  179.1 6.1 concatenate.74
  185.2 4.8 concatenate.75
  190.0 6.1 concatenate.76
  219.3 13.8 fusion.98
  233.7 9.7 all-gather.14.cloned.1.call-done
  243.4 8.0 convolution_convert_fusion
  252.9 19.2 %reduce-scatter.6.cloned.1.call-done = bf16[3136,1024]{1,0:T(8,128)(2,1)} async-done(((bf16[3136,2048]{1,0:T(8,128)(2,1)}), bf16[3136,1024]{1,0:T(8,128)(2,1)}) %reduce-scatter.6.cloned.1.call-update) | async-done | bytes 6422544 | tf_op jit(solution)/shard_map/reduce_scatter | solution.py:170
  278.5 10.2 fusion.18
  288.7 12.1 reshape.266
  300.9 7.5 reduce_sum.235
  313.3 7.1 broadcast_in_dim.10
  320.4 12.3 reshape.267
  332.7 14.1 fusion.12
  346.8 5.3 fusion.11
  352.3 26.4 %all-gather.16.cloned.1.call-done = bf16[3136,2048]{1,0:T(8,128)(2,1)} async-done(((bf16[3136,1024]{1,0:T(8,128)(2,1)}), bf16[3136,2048]{1,0:T(8,128)(2,1)}) %all-gather.16.cloned.1.call-update) | async-done | bytes 12845072 | tf_op jit(solution)/shard_map/all_gather | solution.py:197
  378.7 9.1 multiply_reduce_fusion.1
  389.8 20.9 %fusion.99 = f32[3136,4608]{1,0:T(8,128)} fusion(bf16[3136,256]{1,0:T(8,128)(2,1)S(1)} %multiply_convert_fusion.1, bf16[4608,256]{1,0:T(8,128)(2,1)S(1)} %copy-done.34), kind=kOutput, calls=%fused_computation.213 | convolution fusion | flops 7398752256 | bytes 61767680 | tf_op jit(solution)/shard_map/dot_general | solution.py:77
  410.7 70.2 %reshape.268 = f32[64,7,7,9,512]{4,3,2,1,0:T(8,128)} reshape(f32[3136,4608]{1,0:T(8,128)} %fusion.99) | data formatting | bytes 115605504 | tf_op jit(solution)/shard_map/reshape | solution.py:39
  481.0 159.8 %fusion.93 = (f32[64,7,7,1,512]{4,3,2,1,0:T(1,128)}, f32[64,7,7,1,512]{4,3,2,1,0:T(1,128)}, f32[64,7,7,1,512]{4,3,2,1,0:T(1,128)}, f32[64,7,7,1,512]{4,3,2,1,0:T...) fusion(f32[64,7,7,9,512]{4,3,2,1,0:T(8,128)} %reshape.268), kind=kLoop, calls=%fused_computation.207 | loop fusion | bytes 115605504 | tf_op jit(solution)/shard_map/slice | solution.py:44
  640.8 6.7 copy.388
  681.8 8.1 pad_add_fusion
  689.9 12.3 fusion.19
  702.2 5.5 copy.341
  707.7 6.8 convert_element_type.152
  714.6 8.7 fusion.88
  723.4 16.1 fusion.100
  744.8 8.7 fusion.20
  753.6 57.6 %reduce-scatter.14.cloned.1.call-done = f32[128,256]{1,0:T(8,128)} async-done(((f32[2048,256]{1,0:T(8,128)}), f32[128,256]{1,0:T(8,128)}) %reduce-scatter.14.cloned.1.call-update) | async-done | bytes 131088 | tf_op jit(solution)/shard_map/reduce_scatter | solution.py:216
  815.9 135.8 %reduce-scatter.12.cloned.1.call-done = f32[288,256]{1,0:T(8,128)} async-done(((f32[4608,256]{1,0:T(8,128)}), f32[288,256]{1,0:T(8,128)}) %reduce-scatter.12.cloned.1.call-update) | async-done | bytes 294928 | tf_op jit(solution)/shard_map/reduce_scatter | solution.py:215
  956.5 77.3 %reduce-scatter.10.cloned.1.call-done = f32[128,256]{0,1:T(8,128)} async-done(((f32[2048,256]{0,1:T(8,128)}), f32[128,256]{0,1:T(8,128)}) %reduce-scatter.10.cloned.1.call-update) | async-done | bytes 131088 | tf_op jit(solution)/shard_map/reduce_scatter | solution.py:214
  1045.3 135.8 %all-reduce.30.cloned.1.call-done = (f32[512,512]{1,0:T(8,128)}, f32[512,512]{1,0:T(8,128)}, f32[512,512]{1,0:T(8,128)}) async-done(((f32[512,512]{1,0:T(8,128)}, f32[512,512]{1,0:T(8,128)}, f32[512,512]{1,0:T(8,128)}), (f32[512,512]{1,0:T(8,128)}, f32[512,512]{1,0:T(8,128)}, f32[512,512]{1,0:T(8,128)})) %all-reduce.30.cloned.1.call-update) | async-done | bytes 3145744 | tf_op jit(solution)/shard_map/psum | solution.py:87
  1200.2 138.0 %all-reduce.28.cloned.1.call-done = (f32[512,512]{1,0:T(8,128)}, f32[512,512]{1,0:T(8,128)}, f32[512,512]{1,0:T(8,128)}) async-done(((f32[512,512]{1,0:T(8,128)}, f32[512,512]{1,0:T(8,128)}, f32[512,512]{1,0:T(8,128)}), (f32[512,512]{1,0:T(8,128)}, f32[512,512]{1,0:T(8,128)}, f32[512,512]{1,0:T(8,128)})) %all-reduce.28.cloned.1.call-update) | async-done | bytes 3145744 | tf_op jit(solution)/shard_map/psum | solution.py:87
  1351.8 137.8 %all-reduce.26.cloned.1.call-done = (f32[512,512]{1,0:T(8,128)}, f32[512,512]{1,0:T(8,128)}, f32[512,512]{1,0:T(8,128)}) async-done(((f32[512,512]{1,0:T(8,128)}, f32[512,512]{1,0:T(8,128)}, f32[512,512]{1,0:T(8,128)}), (f32[512,512]{1,0:T(8,128)}, f32[512,512]{1,0:T(8,128)}, f32[512,512]{1,0:T(8,128)})) %all-reduce.26.cloned.1.call-update) | async-done | bytes 3145744 | tf_op jit(solution)/shard_map/psum | solution.py:87
  1503.4 137.7 %all-reduce.24.cloned.1.call-done = (f32[512,512]{1,0:T(8,128)}, f32[512,512]{1,0:T(8,128)}, f32[512,512]{1,0:T(8,128)}) async-done(((f32[512,512]{1,0:T(8,128)}, f32[512,512]{1,0:T(8,128)}, f32[512,512]{1,0:T(8,128)}), (f32[512,512]{1,0:T(8,128)}, f32[512,512]{1,0:T(8,128)}, f32[512,512]{1,0:T(8,128)})) %all-reduce.24.cloned.1.call-update) | async-done | bytes 3145744 | tf_op jit(solution)/shard_map/psum | solution.py:87
  1655.9 42.4 %all-reduce.15 = (f32[1]{0:T(128)}, f32[1]{0:T(128)}) all-reduce(f32[1]{0:T(128)} %bitcast.17, f32[1]{0:T(128)} %bitcast.16), channel_id=1, replica_groups=mesh['client'=16,'chan'=2] {'client'}, use_global_device_ids=true, to_apply=%region_14.15 | all-reduce | flops 2 | bytes 16 | tf_op jit(solution)/shard_map/psum | solution.py:185
  1708.8 83.9 %all-reduce.22.cloned.1.call-done = (f32[512,512]{1,0:T(8,128)}, f32[512,512]{1,0:T(8,128)}, f32[512,512]{1,0:T(8,128)}) async-done(((f32[512,512]{1,0:T(8,128)}, f32[512,512]{1,0:T(8,128)}, f32[512,512]{1,0:T(8,128)}), (f32[512,512]{1,0:T(8,128)}, f32[512,512]{1,0:T(8,128)}, f32[512,512]{1,0:T(8,128)})) %all-reduce.22.cloned.1.call-update) | async-done | bytes 3145744 | tf_op jit(solution)/shard_map/psum | solution.py:87
  (386 shorter events, 193.1 us)
Async XLA Ops:
  7.2 63.8 %all-gather.8.cloned.1.call-start = ((), (), s32[]{:S(2)}) async-start(), calls=%async_computation.11 | async-start | bytes 1114112 | tf_op jit(solution)/shard_map/all_gather | solution.py:153
  12.9 83.7 %all-gather.18.cloned.1.call-start = ((), (), s32[]{:S(2)}) async-start(), calls=%async_computation.21 | async-start | bytes 19267584 | tf_op jit(solution)/shard_map/all_gather | solution.py:161
  13.6 106.8 %all-gather.10.cloned.1.call-start = ((), (), s32[]{:S(2)}) async-start(), calls=%async_computation.12 | async-start | bytes 4816896 | tf_op jit(solution)/shard_map/all_gather | solution.py:165
  13.7 90.3 %copy-start.59 = (f32[1,256]{1,0:T(1,128)}, f32[1,256]{1,0:T(1,128)S(1)}, u32[]{:S(2)}) copy-start(f32[1,256]{1,0:T(1,128)S(1)} %get-tuple-element.197) | copy-start | bytes 3076
  13.7 90.3 %copy-start.65 = (f32[1,256]{1,0:T(1,128)}, f32[1,256]{1,0:T(1,128)S(1)}, u32[]{:S(2)}) copy-start(f32[1,256]{1,0:T(1,128)S(1)} %get-tuple-element.196) | copy-start | bytes 3076
  13.7 364.9 %copy-start.83 = (f32[1,256]{1,0:T(1,128)}, f32[1,256]{1,0:T(1,128)S(1)}, u32[]{:S(2)}) copy-start(f32[1,256]{1,0:T(1,128)S(1)} %get-tuple-element.195) | copy-start | bytes 3076
  13.8 374.0 %copy-start.73 = (f32[1,256]{1,0:T(1,128)}, f32[1,256]{1,0:T(1,128)S(1)}, u32[]{:S(2)}) copy-start(f32[1,256]{1,0:T(1,128)S(1)} %get-tuple-element.194) | copy-start | bytes 3076
  107.4 111.9 %all-gather.12.cloned.1.call-start = ((), (), s32[]{:S(2)}) async-start(), calls=%async_computation.13 | async-start | bytes 2506752 | tf_op jit(solution)/shard_map/all_gather | solution.py:154
  112.1 131.2 %all-gather.14.cloned.1.call-start = ((), (), s32[]{:S(2)}) async-start(), calls=%async_computation.14 | async-start | bytes 1114112 | tf_op jit(solution)/shard_map/all_gather | solution.py:155
  116.7 155.4 %reduce-scatter.6.cloned.1.call-start = ((), (), s32[]{:S(2)}) async-start(), calls=%async_computation.15 | async-start | bytes 19267584 | tf_op jit(solution)/shard_map/reduce_scatter | solution.py:170
  233.2 154.6 %copy-start.67 = (f32[256]{0:T(256)}, f32[256]{0:T(256)S(1)}, u32[]{:S(2)}) copy-start(f32[256]{0:T(256)S(1)} %broadcast_multiply_fusion.7) | copy-start | bytes 3076
  233.6 154.1 %copy-start.71 = (f32[256]{0:T(256)}, f32[256]{0:T(256)S(1)}, u32[]{:S(2)}) copy-start(f32[256]{0:T(256)S(1)} %add_rsqrt_fusion.1) | copy-start | bytes 3076
  251.4 127.3 %all-gather.16.cloned.1.call-start = ((), (), s32[]{:S(2)}) async-start(), calls=%async_computation.16 | async-start | bytes 19267584 | tf_op jit(solution)/shard_map/all_gather | solution.py:197
  320.4 26.4 %slice-start = ((s8[6422528]{0:T(1024)(128)(4,1)}), s8[2228224]{0:T(1024)(128)(4,1)S(1)}, s32[]{:S(2)}) async-start(s8[6422528]{0:T(1024)(128)(4,1)} %bitcast.188), calls=%async_computation.27 | async-start | bytes 4456448
  352.1 26.6 %copy-start.4 = (f32[3136,256]{1,0:T(8,128)S(1)}, f32[3136,256]{1,0:T(8,128)}, u32[]{:S(2)}) copy-start(f32[3136,256]{1,0:T(8,128)} %copy-done.3) | copy-start | bytes 9633796
  352.1 387.5 %reduce-scatter.8.cloned.1.call-start = ((), (), s32[]{:S(2)}) async-start(), calls=%async_computation.17 | async-start | bytes 4816896 | tf_op jit(solution)/shard_map/reduce_scatter | solution.py:206
  714.5 96.7 %reduce-scatter.14.cloned.1.call-start = ((), (), s32[]{:S(2)}) async-start(), calls=%async_computation.20 | async-start | bytes 2228224 | tf_op jit(solution)/shard_map/reduce_scatter | solution.py:216
  723.4 228.3 %reduce-scatter.12.cloned.1.call-start = ((), (), s32[]{:S(2)}) async-start(), calls=%async_computation.19 | async-start | bytes 5013504 | tf_op jit(solution)/shard_map/reduce_scatter | solution.py:215
  739.5 294.3 %reduce-scatter.10.cloned.1.call-start = ((), (), s32[]{:S(2)}) async-start(), calls=%async_computation.18 | async-start | bytes 2228224 | tf_op jit(solution)/shard_map/reduce_scatter | solution.py:214
  753.5 285.3 %copy-start.15 = (f32[1,272,512]{2,1,0:T(8,128)S(1)}, f32[1,272,512]{2,1,0:T(8,128)}, u32[]{:S(2)}) copy-start(f32[1,272,512]{2,1,0:T(8,128)} %param.15) | copy-start | bytes 1671172
  753.5 285.3 %copy-start.35 = (f32[1,272,512]{2,1,0:T(8,128)S(1)}, f32[1,272,512]{2,1,0:T(8,128)}, u32[]{:S(2)}) copy-start(f32[1,272,512]{2,1,0:T(8,128)} %param.16) | copy-start | bytes 1671172
  753.5 285.3 %copy-start.37 = (f32[1,272,512]{2,1,0:T(8,128)S(1)}, f32[1,272,512]{2,1,0:T(8,128)}, u32[]{:S(2)}) copy-start(f32[1,272,512]{2,1,0:T(8,128)} %param.17) | copy-start | bytes 1671172
  753.5 427.5 %all-reduce.30.cloned.1.call-start = ((), (), s32[]{:S(2)}) async-start(), calls=%async_computation.26 | async-start | bytes 6291456 | tf_op jit(solution)/shard_map/psum | solution.py:87
  815.9 136.8 %copy-start.45 = (bf16[2,64,256]{2,1,0:T(8,128)(2,1)}, bf16[2,64,256]{2,1,0:T(8,128)(2,1)S(1)}, u32[]{:S(2)}) copy-start(bf16[2,64,256]{2,1,0:T(8,128)(2,1)S(1)} %all_to_all.99) | copy-start | bytes 196612
  956.5 88.7 %copy-start.39 = (bf16[2,144,256]{2,1,0:T(8,128)(2,1)}, bf16[2,144,256]{2,1,0:T(8,128)(2,1)S(1)}, u32[]{:S(2)}) copy-start(bf16[2,144,256]{2,1,0:T(8,128)(2,1)S(1)} %all_to_all.100) | copy-start | bytes 442372
  1045.2 292.9 %all-reduce.28.cloned.1.call-start = ((), (), s32[]{:S(2)}) async-start(), calls=%async_computation.25 | async-start | bytes 6291456 | tf_op jit(solution)/shard_map/psum | solution.py:87
  1195.5 142.6 %copy-start.25 = (f32[64,512]{1,0:T(8,128)S(1)}, f32[64,512]{1,0:T(8,128)}, u32[]{:S(2)}) copy-start(f32[64,512]{1,0:T(8,128)} %copy-done.24) | copy-start | bytes 393220
  1197.9 146.4 %copy-start.26 = (f32[64,512]{1,0:T(8,128)}, f32[64,512]{1,0:T(8,128)S(1)}, u32[]{:S(2)}) copy-start(f32[64,512]{1,0:T(8,128)S(1)} %fusion.35) | copy-start | bytes 393220
  1199.9 289.7 %all-reduce.26.cloned.1.call-start = ((), (), s32[]{:S(2)}) async-start(), calls=%async_computation.24 | async-start | bytes 6291456 | tf_op jit(solution)/shard_map/psum | solution.py:87
  1347.9 141.7 %copy-start.29 = (f32[64,512]{1,0:T(8,128)S(1)}, f32[64,512]{1,0:T(8,128)}, u32[]{:S(2)}) copy-start(f32[64,512]{1,0:T(8,128)} %copy-done.28) | copy-start | bytes 393220
  1351.5 289.7 %all-reduce.24.cloned.1.call-start = ((), (), s32[]{:S(2)}) async-start(), calls=%async_computation.23 | async-start | bytes 6291456 | tf_op jit(solution)/shard_map/psum | solution.py:87
  1499.4 141.7 %copy-start.31 = (f32[64,512]{1,0:T(8,128)S(1)}, f32[64,512]{1,0:T(8,128)}, u32[]{:S(2)}) copy-start(f32[64,512]{1,0:T(8,128)} %copy-done.30) | copy-start | bytes 393220
  1500.9 146.4 %copy-start.32 = (f32[64,512]{1,0:T(8,128)}, f32[64,512]{1,0:T(8,128)S(1)}, u32[]{:S(2)}) copy-start(f32[64,512]{1,0:T(8,128)S(1)} %fusion.37) | copy-start | bytes 393220
  1502.9 289.8 %all-reduce.22.cloned.1.call-start = ((), (), s32[]{:S(2)}) async-start(), calls=%async_computation.22 | async-start | bytes 6291456 | tf_op jit(solution)/shard_map/psum | solution.py:87
  1650.9 47.4 %copy-start.42 = (f32[64,1024]{1,0:T(8,128)S(1)}, f32[64,1024]{1,0:T(8,128)}, u32[]{:S(2)}) copy-start(f32[64,1024]{1,0:T(8,128)} %copy-done.41) | copy-start | bytes 786436
  1650.9 47.4 %copy-start.49 = (f32[64,100]{1,0:T(8,128)S(1)}, f32[64,100]{1,0:T(8,128)}, u32[]{:S(2)}) copy-start(f32[64,100]{1,0:T(8,128)} %copy-done.48) | copy-start | bytes 76804
  1650.9 47.4 %copy-start.78 = (s32[1,64]{1,0:T(1,128)S(1)}, s32[1,64]{1,0:T(1,128)}, u32[]{:S(2)}) copy-start(s32[1,64]{1,0:T(1,128)} %param.13) | copy-start | bytes 772
  1650.9 47.4 %copy-start.80 = (f32[64]{0:T(128)S(1)}, f32[64]{0:T(128)}, u32[]{:S(2)}) copy-start(f32[64]{0:T(128)} %copy-done.79) | copy-start | bytes 772
  1654.5 51.2 %copy-start.46 = (bf16[2,64,256]{2,1,0:T(8,128)(2,1)S(1)}, bf16[2,64,256]{2,1,0:T(8,128)(2,1)}, u32[]{:S(2)}) copy-start(bf16[2,64,256]{2,1,0:T(8,128)(2,1)} %copy-done.45) | copy-start | bytes 196612
  1654.5 51.9 %copy-start.61 = (f32[1024]{0:T(1024)S(1)}, f32[1024]{0:T(1024)}, u32[]{:S(2)}) copy-start(f32[1024]{0:T(1024)} %get-tuple-element.130) | copy-start | bytes 12292
  1654.5 51.9 %copy-start.62 = (f32[1024]{0:T(1024)S(1)}, f32[1024]{0:T(1024)}, u32[]{:S(2)}) copy-start(f32[1024]{0:T(1024)} %get-tuple-element.133) | copy-start | bytes 12292
  1654.5 51.9 %copy-start.81 = (f32[256]{0:T(256)S(1)}, f32[256]{0:T(256)}, u32[]{:S(2)}) copy-start(f32[256]{0:T(256)} %get-tuple-element.136) | copy-start | bytes 3076
  1654.5 51.9 %copy-start.82 = (f32[256]{0:T(256)S(1)}, f32[256]{0:T(256)}, u32[]{:S(2)}) copy-start(f32[256]{0:T(256)} %get-tuple-element.141) | copy-start | bytes 3076
  1654.5 52.0 %copy-start.54 = (f32[1,2,1,1536]{3,2,1,0:T(1,128)S(1)}, f32[1,2,1,1536]{3,2,1,0:T(1,128)}, u32[]{:S(2)}) copy-start(f32[1,2,1,1536]{3,2,1,0:T(1,128)} %param.18) | copy-start | bytes 36868
  1654.5 52.0 %copy-start.63 = (f32[1,2,1,1536]{3,2,1,0:T(1,128)S(1)}, f32[1,2,1,1536]{3,2,1,0:T(1,128)}, u32[]{:S(2)}) copy-start(f32[1,2,1,1536]{3,2,1,0:T(1,128)} %param.19) | copy-start | bytes 36868
  1654.5 52.0 %copy-start.64 = (f32[1,2,1,1536]{3,2,1,0:T(1,128)S(1)}, f32[1,2,1,1536]{3,2,1,0:T(1,128)}, u32[]{:S(2)}) copy-start(f32[1,2,1,1536]{3,2,1,0:T(1,128)} %param.20) | copy-start | bytes 36868
  1654.6 52.6 %copy-start.40 = (bf16[2,144,256]{2,1,0:T(8,128)(2,1)S(1)}, bf16[2,144,256]{2,1,0:T(8,128)(2,1)}, u32[]{:S(2)}) copy-start(bf16[2,144,256]{2,1,0:T(8,128)(2,1)} %copy-done.39) | copy-start | bytes 442372
  1654.6 53.5 %copy-start.44 = (bf16[2,64,256]{2,1,0:T(8,128)(2,1)S(1)}, bf16[2,64,256]{2,1,0:T(8,128)(2,1)}, u32[]{:S(2)}) copy-start(bf16[2,64,256]{2,1,0:T(8,128)(2,1)} %copy-done.43) | copy-start | bytes 196612
  (73 other events, 369.0 us)
Sparse Core Ops, SparseCore 0:
  13.0 57.9 all-gather.7
  72.6 23.9 all-gather.17
  107.5 12.8 all-gather.9
  123.1 63.4 all-gather.11
  189.2 54.0 all-gather.13
  251.5 20.5 reduce-scatter.5
  352.2 26.4 all-gather.15
  714.6 12.1 reduce-scatter.7
  729.2 81.9 reduce-scatter.13
  817.0 134.6 reduce-scatter.11
  954.0 79.8 reduce-scatter.9
  1045.3 135.6 all-reduce.29
  1200.0 138.0 all-reduce.27
  1351.6 137.9 all-reduce.25
  1503.0 138.0 all-reduce.23
  1654.6 138.0 all-reduce.21
where the time goes:
time: 1820 us; the launch traced here: 1810 us
  waiting for transfers between devices  1050 us (58%)
  local copies, waits for them, and re-layouts  425 us (23%)
  matrix products  162 us (9%)
  other arithmetic  83.6 us (5%)
  blocking collectives  70.9 us (4%)
  between operations  18.9 us (1%)
    psum x5, waiting for transfers between devices, gram_sum(): lax.psum((gram_of(first_part), gram_of(middle_part), gram_of(last_part)),...  633 us
    slice x10, local copies, waits for them, and re-layouts, fold_patches(): columns[:, :, :, 3 * shift_y + shift_x, :]  198 us
    reduce_scatter x1, waiting for transfers between devices, on_device(): lax.psum_scatter(grad_middle, 'client', scatter_dimension=0, tiled=True)  136 us
    reduce_scatter x1, waiting for transfers between devices, on_device(): lax.psum_scatter(grad_reduce, 'client', scatter_dimension=0, tiled=True)  77.3 us
    reshape x1, local copies, waits for them, and re-layouts, fold_patches(): columns = grads.reshape(images, 7, 7, 9, width)  70.2 us
    reduce_scatter x1, waiting for transfers between devices, on_device(): lax.psum_scatter(grad_expand, 'client', scatter_dimension=0, tiled=True)  57.6 us
    all_gather x1, waiting for transfers between devices, on_device(): lax.all_gather(first_piece, 'client', axis=0, tiled=True)  57.2 us
    concatenate x9, local copies, waits for them, and re-layouts, patches_of(): return jnp.concatenate(taps, axis=-1).reshape(images * 49, 9 * width)  48.3 us
  transfers between devices with their start and end apart: 16, of which 14 were waited for; matrix products, arithmetic and copies ran while one was open for 9% of the time, Pallas kernels for 0%

commit v1 on v0

--- a/solution.py
+++ b/solution.py
@@ -89,13 +89,12 @@
     )
 
 
-def schulz_step(current, gram):
-    product = jnp.dot(current, gram, precision=precise)
-    return (
-        schulz_first * current
-        + schulz_second * product
-        + schulz_third * jnp.dot(product, gram, precision=precise)
-    )
+def square(gram):
+    return jnp.dot(gram, gram, precision=precise)
+
+
+def times_poly(left, mixed):
+    return schulz_first * left + jnp.dot(left, mixed, precision=precise)
 
 
 def adam_update(param, grad, first, second, rate, decay):
@@ -240,9 +239,12 @@
     current = [sections[slot] * factors[slot] for slot in range(3)]
     grams = [raw_grams[slot] * (factors[slot] * factors[slot]) for slot in range(3)]
     for turn in range(NS_STEPS):
-        if turn > 0:
-            grams = gram_sum(current[0], current[1], current[2])
-        current = [schulz_step(current[slot], grams[slot]) for slot in range(3)]
+        mixed = [schulz_second * gram + schulz_third * square(gram) for gram in grams]
+        current = [times_poly(current[slot], mixed[slot]) for slot in range(3)]
+        if turn + 1 < NS_STEPS:
+            grams = [
+                times_poly(times_poly(grams[slot], mixed[slot]), mixed[slot]) for slot in range(3)
+            ]
     ratio = (channels / width) ** 0.5
     ortho = jnp.concatenate([current[0] * ratio, current[1] * 3.0, current[2] * ratio], axis=0)
     base_new = master - muon_rate * (ortho + muon_decay * master)

time: 1820 us -> 1300 us (0.71)
  waiting for transfers between devices: 1050 us -> 497 us
  matrix products: 162 us -> 198 us
    psum x5 -> x1, waiting for transfers between devices: 633 us -> 85.1 us  [gram_sum(): lax.psum((gram_of(first_part), gram_of(middle_part), gram_of(last_part)),...]
    dot_general x30 -> x54, matrix products: 37 us -> 97.2 us  [the longest x39 64 us: times_poly(): return schulz_first * left + jnp.dot(left, mixed, precision=precise)]
    dot_general x15 -> x3, matrix products: 30.5 us -> 6.12 us  [gram_of(): lax.dot_general(section, section, (((0,), (0,)), ((), ())), precision=pre...]
  transfers between devices with their start and end apart: 16 -> 12, of which waited for: 14 -> 10; matrix products, arithmetic and copies ran while one was open for 9% -> 12% of each run, Pallas kernels for 0% -> 0%
where the time goes in v1:
time: 1300 us; the launch traced here: 1290 us
  waiting for transfers between devices  497 us (38%)
  local copies, waits for them, and re-layouts  426 us (33%)
  matrix products  198 us (15%)
  other arithmetic  83.9 us (6%)
  blocking collectives  68.3 us (5%)
  between operations  19.4 us (1%)
    slice x10, local copies, waits for them, and re-layouts, fold_patches(): columns[:, :, :, 3 * shift_y + shift_x, :]  198 us
    reduce_scatter x1, waiting for transfers between devices, on_device(): lax.psum_scatter(grad_middle, 'client', scatter_dimension=0, tiled=True)  136 us
    psum x1, waiting for transfers between devices, gram_sum(): lax.psum((gram_of(first_part), gram_of(middle_part), gram_of(last_part)),...  85.1 us
    reduce_scatter x1, waiting for transfers between devices, on_device(): lax.psum_scatter(grad_reduce, 'client', scatter_dimension=0, tiled=True)  77.5 us
    reshape x1, local copies, waits for them, and re-layouts, fold_patches(): columns = grads.reshape(images, 7, 7, 9, width)  70.3 us
    dot_general x39, matrix products, times_poly(): return schulz_first * left + jnp.dot(left, mixed, precision=precise)  64 us
    all_gather x1, waiting for transfers between devices, on_device(): lax.all_gather(first_piece, 'client', axis=0, tiled=True)  57.2 us
    reduce_scatter x1, waiting for transfers between devices, on_device(): lax.psum_scatter(grad_expand, 'client', scatter_dimension=0, tiled=True)  57.2 us
  transfers between devices with their start and end apart: 12, of which 10 were waited for; matrix products, arithmetic and copies ran while one was open for 12% of the time, Pallas kernels for 0%

profile of v1, /device:TPU:0, one launch (start us, length us, event | category | flops | bytes accessed | tf_op | source)
XLA Modules:
  0.0 1293.3 jit_solution(10974480412677627002)
XLA Ops:
  8.4 4.5 all_to_all.96
  13.8 57.2 %all-gather.8.cloned.1.call-done = bf16[2048,256]{1,0:T(8,128)(2,1)} async-done(((bf16[128,256]{1,0:T(8,128)(2,1)}), bf16[2048,256]{1,0:T(8,128)(2,1)}) %all-gather.8.cloned.1.call-update) | async-done | bytes 1048592 | tf_op jit(solution)/shard_map/all_gather | solution.py:152
  71.0 25.6 %all-gather.18.cloned.1.call-done = bf16[1,3136,2048]{2,1,0:T(8,128)(2,1)} async-done(((bf16[1,3136,1024]{2,1,0:T(8,128)(2,1)}), bf16[1,3136,2048]{2,1,0:T(8,128)(2,1)}) %all-gather.18.cloned.1.call-update) | async-done | bytes 12845072 | tf_op jit(solution)/shard_map/all_gather | solution.py:160
  96.6 6.9 fusion.100
  107.5 4.6 all_to_all.97
  112.2 4.5 all_to_all.98
  120.4 6.1 reshape.265
  126.5 22.0 %pad_slice_fusion = (bf16[64,7,7,512]{3,2,1,0:T(8,128)(2,1)}, bf16[64,7,7,512]{3,2,1,0:T(8,128)(2,1)}, bf16[64,7,7,512]{3,2,1,0:T(8,128)(2,1)}, bf16[64,7,7,512]...) fusion(bf16[64,7,7,512]{3,2,1,0:T(8,128)(2,1)} %reshape.265), kind=kLoop, calls=%fused_computation | loop fusion | bytes 28901376 | tf_op jit(solution)/shard_map/slice | solution.py:31
  148.6 4.8 concatenate.69
  155.4 6.1 concatenate.70
  161.5 6.1 concatenate.71
  167.6 6.3 concatenate.72
  173.9 6.1 concatenate.73
  180.1 6.1 concatenate.74
  186.2 4.8 concatenate.75
  191.0 6.1 concatenate.76
  220.4 13.8 %fusion.101 = (f32[256]{0:T(256)S(1)}, f32[3136,256]{1,0:T(8,128)S(1)}) fusion(bf16[3136,4608]{1,0:T(8,128)(2,1)} %constant_dynamic-update-slice_fusion, bf16[4608,256]{1,0:T(8,128)(2,1)} %all-gather.12.cloned.1.call-done), kind=kOutput, calls=%fused_computation.251 | convolution fusion | flops 7399555072 | bytes 34472960 | tf_op jit(solution)/shard_map/dot_general | solution.py:166
  234.7 8.7 all-gather.14.cloned.1.call-done
  243.3 8.0 convolution_convert_fusion
  252.9 19.2 %reduce-scatter.6.cloned.1.call-done = bf16[3136,1024]{1,0:T(8,128)(2,1)} async-done(((bf16[3136,2048]{1,0:T(8,128)(2,1)}), bf16[3136,1024]{1,0:T(8,128)(2,1)}) %reduce-scatter.6.cloned.1.call-update) | async-done | bytes 6422544 | tf_op jit(solution)/shard_map/reduce_scatter | solution.py:169
  278.5 10.3 fusion.18
  288.7 12.2 reshape.266
  300.9 7.5 reduce_sum.235
  313.3 7.1 broadcast_in_dim.10
  320.4 12.4 reshape.267
  332.8 14.1 %fusion.12 = (f32[1024]{0:T(1024)}, f32[1024]{0:T(1024)S(1)}, f32[1024]{0:T(1024)S(1)}, f32[1024]{0:T(1024)}, f32[3136,1024]{1,0:T(8,128)S(1)}) fusion(bf16[3136,1024]{1,0:T(8,128)(2,1)} %reduce-scatter.6.cloned.1.call-done, f32[1024]{0:T(1024)S(1)} %add_rsqrt_fusion, f32[1024]{0:T(1024)S(1)} %broadcast_multiply_fusion.2, f32[1024]{0:T(1024)S(1)} %bitcast.254, ...), kind=kLoop, calls=%fused_computation.23 | loop fusion | flops 70643712 | bytes 38567936 | tf_op jit(solution)/shard_map/reduce_sum | solution.py:62
  346.9 5.4 fusion.11
  352.6 26.4 %all-gather.16.cloned.1.call-done = bf16[3136,2048]{1,0:T(8,128)(2,1)} async-done(((bf16[3136,1024]{1,0:T(8,128)(2,1)}), bf16[3136,2048]{1,0:T(8,128)(2,1)}) %all-gather.16.cloned.1.call-update) | async-done | bytes 12845072 | tf_op jit(solution)/shard_map/all_gather | solution.py:196
  378.9 9.1 multiply_reduce_fusion.1
  390.0 20.8 %fusion.102 = f32[3136,4608]{1,0:T(8,128)} fusion(bf16[3136,256]{1,0:T(8,128)(2,1)S(1)} %multiply_convert_fusion.1, bf16[4608,256]{1,0:T(8,128)(2,1)S(1)} %copy-done.21), kind=kOutput, calls=%fused_computation.252 | convolution fusion | flops 7398752256 | bytes 61767680 | tf_op jit(solution)/shard_map/dot_general | solution.py:77
  410.8 70.3 %reshape.268 = f32[64,7,7,9,512]{4,3,2,1,0:T(8,128)} reshape(f32[3136,4608]{1,0:T(8,128)} %fusion.102) | data formatting | bytes 115605504 | tf_op jit(solution)/shard_map/reshape | solution.py:39
  481.1 159.8 %fusion.96 = (f32[64,7,7,1,512]{4,3,2,1,0:T(1,128)}, f32[64,7,7,1,512]{4,3,2,1,0:T(1,128)}, f32[64,7,7,1,512]{4,3,2,1,0:T(1,128)}, f32[64,7,7,1,512]{4,3,2,1,0:T...) fusion(f32[64,7,7,9,512]{4,3,2,1,0:T(8,128)} %reshape.268), kind=kLoop, calls=%fused_computation.246 | loop fusion | bytes 115605504 | tf_op jit(solution)/shard_map/slice | solution.py:44
  640.9 6.7 copy.388
  647.7 4.2 copy.389
  656.2 4.2 copy.391
  682.0 8.1 pad_add_fusion
  690.1 12.3 fusion.19
  702.4 5.5 copy.341
  707.9 6.8 convert_element_type.152
  714.9 8.8 fusion.91
  723.8 16.1 %fusion.103 = f32[4608,256]{1,0:T(8,128)} fusion(bf16[3136,4608]{1,0:T(8,128)(2,1)} %constant_dynamic-update-slice_fusion, bf16[3136,256]{1,0:T(8,128)(2,1)} %copy-done.15), kind=kOutput, calls=%fused_computation.253 | convolution fusion | flops 7398752256 | bytes 35225600 | tf_op jit(solution)/shard_map/dot_general | solution.py:71
  745.2 8.7 fusion.20
  754.0 57.2 %reduce-scatter.14.cloned.1.call-done = f32[128,256]{1,0:T(8,128)} async-done(((f32[2048,256]{1,0:T(8,128)}), f32[128,256]{1,0:T(8,128)}) %reduce-scatter.14.cloned.1.call-update) | async-done | bytes 131088 | tf_op jit(solution)/shard_map/reduce_scatter | solution.py:215
  815.9 135.8 %reduce-scatter.12.cloned.1.call-done = f32[288,256]{1,0:T(8,128)} async-done(((f32[4608,256]{1,0:T(8,128)}), f32[288,256]{1,0:T(8,128)}) %reduce-scatter.12.cloned.1.call-update) | async-done | bytes 294928 | tf_op jit(solution)/shard_map/reduce_scatter | solution.py:214
  956.5 77.5 %reduce-scatter.10.cloned.1.call-done = f32[128,256]{0,1:T(8,128)} async-done(((f32[2048,256]{0,1:T(8,128)}), f32[128,256]{0,1:T(8,128)}) %reduce-scatter.10.cloned.1.call-update) | async-done | bytes 131088 | tf_op jit(solution)/shard_map/reduce_scatter | solution.py:213
  1046.7 39.9 %all-reduce.11 = (f32[1]{0:T(128)}, f32[1]{0:T(128)}) all-reduce(f32[1]{0:T(128)} %bitcast.17, f32[1]{0:T(128)} %bitcast.16), channel_id=1, replica_groups=mesh['client'=16,'chan'=2] {'client'}, use_global_device_ids=true, to_apply=%region_14.15 | all-reduce | flops 2 | bytes 16 | tf_op jit(solution)/shard_map/psum | solution.py:184
  1096.3 85.1 %all-reduce.14.cloned.1.call-done = (f32[512,512]{1,0:T(8,128)}, f32[512,512]{1,0:T(8,128)}, f32[512,512]{1,0:T(8,128)}) async-done(((f32[512,512]{1,0:T(8,128)}, f32[512,512]{1,0:T(8,128)}, f32[512,512]{1,0:T(8,128)}), (f32[512,512]{1,0:T(8,128)}, f32[512,512]{1,0:T(8,128)}, f32[512,512]{1,0:T(8,128)})) %all-reduce.14.cloned.1.call-update) | async-done | bytes 3145744 | tf_op jit(solution)/shard_map/psum | solution.py:87
  1201.0 4.5 convolution_add_fusion.15
  (352 shorter events, 209.6 us)
Async XLA Ops:
  7.2 63.9 %all-gather.8.cloned.1.call-start = ((), (), s32[]{:S(2)}) async-start(), calls=%async_computation.11 | async-start | bytes 1114112 | tf_op jit(solution)/shard_map/all_gather | solution.py:152
  12.9 83.7 %all-gather.18.cloned.1.call-start = ((), (), s32[]{:S(2)}) async-start(), calls=%async_computation.21 | async-start | bytes 19267584 | tf_op jit(solution)/shard_map/all_gather | solution.py:160
  13.7 106.8 %all-gather.10.cloned.1.call-start = ((), (), s32[]{:S(2)}) async-start(), calls=%async_computation.12 | async-start | bytes 4816896 | tf_op jit(solution)/shard_map/all_gather | solution.py:164
  13.7 90.3 %copy-start.41 = (f32[1,256]{1,0:T(1,128)}, f32[1,256]{1,0:T(1,128)S(1)}, u32[]{:S(2)}) copy-start(f32[1,256]{1,0:T(1,128)S(1)} %get-tuple-element.185) | copy-start | bytes 3076
  13.8 90.3 %copy-start.47 = (f32[1,256]{1,0:T(1,128)}, f32[1,256]{1,0:T(1,128)S(1)}, u32[]{:S(2)}) copy-start(f32[1,256]{1,0:T(1,128)S(1)} %get-tuple-element.184) | copy-start | bytes 3076
  13.8 365.2 %copy-start.65 = (f32[1,256]{1,0:T(1,128)}, f32[1,256]{1,0:T(1,128)S(1)}, u32[]{:S(2)}) copy-start(f32[1,256]{1,0:T(1,128)S(1)} %get-tuple-element.183) | copy-start | bytes 3076
  13.8 374.2 %copy-start.55 = (f32[1,256]{1,0:T(1,128)}, f32[1,256]{1,0:T(1,128)S(1)}, u32[]{:S(2)}) copy-start(f32[1,256]{1,0:T(1,128)S(1)} %get-tuple-element.182) | copy-start | bytes 3076
  107.4 113.0 %all-gather.12.cloned.1.call-start = ((), (), s32[]{:S(2)}) async-start(), calls=%async_computation.13 | async-start | bytes 2506752 | tf_op jit(solution)/shard_map/all_gather | solution.py:153
  112.1 131.2 %all-gather.14.cloned.1.call-start = ((), (), s32[]{:S(2)}) async-start(), calls=%async_computation.14 | async-start | bytes 1114112 | tf_op jit(solution)/shard_map/all_gather | solution.py:154
  116.7 155.4 %reduce-scatter.6.cloned.1.call-start = ((), (), s32[]{:S(2)}) async-start(), calls=%async_computation.15 | async-start | bytes 19267584 | tf_op jit(solution)/shard_map/reduce_scatter | solution.py:169
  234.2 17.1 %copy-start.3 = (f32[3136,256]{1,0:T(8,128)}, f32[3136,256]{1,0:T(8,128)S(1)}, u32[]{:S(2)}) copy-start(f32[3136,256]{1,0:T(8,128)S(1)} %get-tuple-element.189) | copy-start | bytes 9633796
  234.2 153.8 %copy-start.49 = (f32[256]{0:T(256)}, f32[256]{0:T(256)S(1)}, u32[]{:S(2)}) copy-start(f32[256]{0:T(256)S(1)} %broadcast_multiply_fusion.7) | copy-start | bytes 3076
  234.7 153.3 %copy-start.53 = (f32[256]{0:T(256)}, f32[256]{0:T(256)S(1)}, u32[]{:S(2)}) copy-start(f32[256]{0:T(256)S(1)} %add_rsqrt_fusion.1) | copy-start | bytes 3076
  251.3 127.6 %all-gather.16.cloned.1.call-start = ((), (), s32[]{:S(2)}) async-start(), calls=%async_computation.16 | async-start | bytes 19267584 | tf_op jit(solution)/shard_map/all_gather | solution.py:196
  300.9 11.3 copy-start.59
  312.2 8.2 copy-start.51
  313.1 7.4 copy-start.61
  320.4 26.5 %slice-start = ((s8[6422528]{0:T(1024)(128)(4,1)}), s8[2228224]{0:T(1024)(128)(4,1)S(1)}, s32[]{:S(2)}) async-start(s8[6422528]{0:T(1024)(128)(4,1)} %bitcast.209), calls=%async_computation.23 | async-start | bytes 4456448
  332.8 14.1 %slice-start.1 = ((s8[6422528]{0:T(1024)(128)(4,1)}), s8[4194304]{0:T(1024)(128)(4,1)S(1)}, s32[]{:S(2)}) async-start(s8[6422528]{0:T(1024)(128)(4,1)} %bitcast.209), calls=%async_computation.24 | async-start | bytes 8388608
  352.3 26.6 %copy-start.4 = (f32[3136,256]{1,0:T(8,128)S(1)}, f32[3136,256]{1,0:T(8,128)}, u32[]{:S(2)}) copy-start(f32[3136,256]{1,0:T(8,128)} %copy-done.3) | copy-start | bytes 9633796
  352.3 387.6 %reduce-scatter.8.cloned.1.call-start = ((), (), s32[]{:S(2)}) async-start(), calls=%async_computation.17 | async-start | bytes 4816896 | tf_op jit(solution)/shard_map/reduce_scatter | solution.py:205
  707.9 6.9 copy-start.50
  707.9 6.9 copy-start.54
  707.9 7.0 copy-start.56
  707.9 7.0 copy-start.66
  714.8 96.4 %reduce-scatter.14.cloned.1.call-start = ((), (), s32[]{:S(2)}) async-start(), calls=%async_computation.20 | async-start | bytes 2228224 | tf_op jit(solution)/shard_map/reduce_scatter | solution.py:215
  723.7 228.0 %reduce-scatter.12.cloned.1.call-start = ((), (), s32[]{:S(2)}) async-start(), calls=%async_computation.19 | async-start | bytes 5013504 | tf_op jit(solution)/shard_map/reduce_scatter | solution.py:214
  739.9 294.1 %reduce-scatter.10.cloned.1.call-start = ((), (), s32[]{:S(2)}) async-start(), calls=%async_computation.18 | async-start | bytes 2228224 | tf_op jit(solution)/shard_map/reduce_scatter | solution.py:213
  753.9 285.0 %copy-start.17 = (f32[1,272,512]{2,1,0:T(8,128)S(1)}, f32[1,272,512]{2,1,0:T(8,128)}, u32[]{:S(2)}) copy-start(f32[1,272,512]{2,1,0:T(8,128)} %param.15) | copy-start | bytes 1671172
  753.9 285.0 %copy-start.22 = (f32[1,272,512]{2,1,0:T(8,128)S(1)}, f32[1,272,512]{2,1,0:T(8,128)}, u32[]{:S(2)}) copy-start(f32[1,272,512]{2,1,0:T(8,128)} %param.16) | copy-start | bytes 1671172
  753.9 285.0 %copy-start.24 = (f32[1,272,512]{2,1,0:T(8,128)S(1)}, f32[1,272,512]{2,1,0:T(8,128)}, u32[]{:S(2)}) copy-start(f32[1,272,512]{2,1,0:T(8,128)} %param.17) | copy-start | bytes 1671172
  753.9 427.5 %all-reduce.14.cloned.1.call-start = ((), (), s32[]{:S(2)}) async-start(), calls=%async_computation.22 | async-start | bytes 6291456 | tf_op jit(solution)/shard_map/psum | solution.py:87
  1039.1 47.5 %copy-start.27 = (f32[64,1024]{1,0:T(8,128)S(1)}, f32[64,1024]{1,0:T(8,128)}, u32[]{:S(2)}) copy-start(f32[64,1024]{1,0:T(8,128)} %copy-done.26) | copy-start | bytes 786436
  1039.2 47.5 %copy-start.31 = (f32[64,100]{1,0:T(8,128)S(1)}, f32[64,100]{1,0:T(8,128)}, u32[]{:S(2)}) copy-start(f32[64,100]{1,0:T(8,128)} %copy-done.30) | copy-start | bytes 76804
  1039.2 47.5 %copy-start.33 = (f32[1,1024,100]{1,0,2:T(1,128)S(1)}, f32[1,1024,100]{1,0,2:T(1,128)}, u32[]{:S(2)}) copy-start(f32[1,1024,100]{1,0,2:T(1,128)} %param.21) | copy-start | bytes 1228804
  1039.2 47.5 %copy-start.60 = (s32[1,64]{1,0:T(1,128)S(1)}, s32[1,64]{1,0:T(1,128)}, u32[]{:S(2)}) copy-start(s32[1,64]{1,0:T(1,128)} %param.13) | copy-start | bytes 772
  1039.2 47.5 %copy-start.62 = (f32[64]{0:T(128)S(1)}, f32[64]{0:T(128)}, u32[]{:S(2)}) copy-start(f32[64]{0:T(128)} %copy-done.61) | copy-start | bytes 772
  1039.2 47.5 %copy-start.67 = (f32[1,1024,100]{1,0,2:T(1,128)S(1)}, f32[1,1024,100]{1,0,2:T(1,128)}, u32[]{:S(2)}) copy-start(f32[1,1024,100]{1,0,2:T(1,128)} %param.22) | copy-start | bytes 1228804
  1045.4 48.5 %copy-start.43 = (f32[1024]{0:T(1024)S(1)}, f32[1024]{0:T(1024)}, u32[]{:S(2)}) copy-start(f32[1024]{0:T(1024)} %get-tuple-element.130) | copy-start | bytes 12292
  1045.4 48.5 %copy-start.44 = (f32[1024]{0:T(1024)S(1)}, f32[1024]{0:T(1024)}, u32[]{:S(2)}) copy-start(f32[1024]{0:T(1024)} %get-tuple-element.133) | copy-start | bytes 12292
  1045.4 48.5 %copy-start.63 = (f32[256]{0:T(256)S(1)}, f32[256]{0:T(256)}, u32[]{:S(2)}) copy-start(f32[256]{0:T(256)} %get-tuple-element.136) | copy-start | bytes 3076
  1045.4 48.5 %copy-start.64 = (f32[256]{0:T(256)S(1)}, f32[256]{0:T(256)}, u32[]{:S(2)}) copy-start(f32[256]{0:T(256)} %get-tuple-element.141) | copy-start | bytes 3076
  1045.4 48.6 %copy-start.36 = (f32[1,2,1,1536]{3,2,1,0:T(1,128)S(1)}, f32[1,2,1,1536]{3,2,1,0:T(1,128)}, u32[]{:S(2)}) copy-start(f32[1,2,1,1536]{3,2,1,0:T(1,128)} %param.18) | copy-start | bytes 36868
  1045.4 48.6 %copy-start.45 = (f32[1,2,1,1536]{3,2,1,0:T(1,128)S(1)}, f32[1,2,1,1536]{3,2,1,0:T(1,128)}, u32[]{:S(2)}) copy-start(f32[1,2,1,1536]{3,2,1,0:T(1,128)} %param.19) | copy-start | bytes 36868
  1045.4 48.6 %copy-start.46 = (f32[1,2,1,1536]{3,2,1,0:T(1,128)S(1)}, f32[1,2,1,1536]{3,2,1,0:T(1,128)}, u32[]{:S(2)}) copy-start(f32[1,2,1,1536]{3,2,1,0:T(1,128)} %param.20) | copy-start | bytes 36868
  1181.5 9.2 copy-start.14
  1181.5 12.0 copy-start.13
  1194.2 11.2 copy-start.12
  (52 other events, 205.8 us)
Sparse Core Ops, SparseCore 0:
  13.0 57.9 all-gather.7
  72.6 23.9 all-gather.17
  107.5 12.8 all-gather.9
  123.1 63.4 all-gather.11
  189.2 54.0 all-gather.13
  251.5 20.5 reduce-scatter.5
  352.5 26.4 all-gather.15
  714.9 12.1 reduce-scatter.7
  729.4 81.7 reduce-scatter.13
  817.1 134.5 reduce-scatter.11
  954.0 80.0 reduce-scatter.9
  1045.5 135.9 all-reduce.13

commit v2 on v1

v2 whole, which is shorter than its diff:
```python
import functools

import jax
import jax.numpy as jnp
from jax import lax
from jax.experimental import pallas as pl
from jax.experimental.pallas import tpu as pltpu
from jax.sharding import PartitionSpec as P

NS_STEPS = 5
STEP = 10

low_type = jnp.bfloat16
wide = jnp.float32
MESH = pl.DeviceIdType.MESH
precise = lax.Precision.HIGHEST
norm_epsilon = 1e-05
prox_weight = 0.05
momentum_decay = 0.95
muon_rate = 0.3
muon_decay = 0.1
schulz_first = 3.4445
schulz_second = -4.775
schulz_third = 2.0315
adam_first = 0.9
adam_second = 0.95
adam_epsilon = 1e-08
head_rate = 0.01
head_decay = 0.05
norm_rate = 0.5

SIDE = 7
PIXELS = SIDE * SIDE
LANES = 128
SPOTS = (4, 2, 2)
VMEM_BYTES = 62 * 2**20


def dot_nn(left, right):
    return jnp.dot(left, right, preferred_element_type=wide)


def dot_nt(left, right):
    return lax.dot_general(left, right, (((1,), (1,)), ((), ())), preferred_element_type=wide)


def dot_tn(left, right):
    return lax.dot_general(left, right, (((0,), (0,)), ((), ())), preferred_element_type=wide)


def flat_rows(block):
    return block.reshape(-1, block.shape[-1])


def sigmoid(value):
    return 0.5 * jnp.tanh(0.5 * value) + 0.5


def fold_rows(value):
    return jnp.sum(value.reshape(value.shape[0] // 8, 8, value.shape[1]), axis=0)


def column_sum(value):
    return jnp.sum(value, axis=0, keepdims=True)


def remote(src, dst, send_sem, recv_sem, client, core):
    return pltpu.make_async_remote_copy(
        src_ref=src,
        dst_ref=dst,
        send_sem=send_sem,
        recv_sem=recv_sem,
        device_id=(client, core),
        device_id_type=MESH,
    )


class Place:
    def __init__(self):
        self.client = lax.axis_index("client")
        self.core = lax.axis_index("chan")
        self.z = self.client // 4
        self.y = (self.client // 2) % 2
        self.x = self.client % 2
        self.others = [
            self.z + 1 - 2 * (self.z % 2),
            (self.z + 2) % 4,
            3 - self.z,
        ]

    def at(self, z, y, x):
        return z * 4 + y * 2 + x

    def along_x(self):
        return self.at(self.z, self.y, 1 - self.x)

    def along_y(self):
        return self.at(self.z, 1 - self.y, self.x)

    def along_z(self, step):
        return self.at(self.others[step], self.y, self.x)

    def greet(self, whole):
        barrier = pltpu.get_barrier_semaphore()
        pairs = [(self.client, 1 - self.core)]
        if whole:
            pairs += [(self.along_x(), self.core), (self.along_y(), self.core)]
            pairs += [(self.along_z(step), self.core) for step in range(3)]
        for pair in pairs:
            pl.semaphore_signal(barrier, inc=1, device_id=pair, device_id_type=MESH)
        pl.semaphore_wait(barrier, len(pairs))


class Spread:
    def __init__(self, place, weights, sems):
        self.place = place
        self.weights = weights
        self.z_sems, self.near_sems, self.far_sems, self.core_sems = sems
        self.order = [place.z] + place.others
        self.copies = []

    def z_copy(self, step, slot):
        p = self.place
        ref = self.weights[slot].at[p.z, p.y, p.x, p.core]
        sems = self.z_sems
        return remote(ref, ref, sems.at[0, step, slot], sems.at[1, step, slot], p.along_z(step), p.core)

    def near_copy(self, turn, slot):
        p = self.place
        ref = self.weights[slot].at[self.order[turn], p.y, p.x, p.core]
        to = p.along_y() if slot == 1 else p.along_x()
        sems = self.near_sems
        return remote(ref, ref, sems.at[0, turn, slot], sems.at[1, turn, slot], to, p.core)

    def far_copy(self, turn, slot):
        p = self.place
        if slot == 1:
            ref, to = self.weights[slot].at[self.order[turn], :, p.x, p.core], p.along_x()
        else:
            ref, to = self.weights[slot].at[self.order[turn], p.y, :, p.core], p.along_y()
        sems = self.far_sems
        return remote(ref, ref, sems.at[0, turn, slot], sems.at[1, turn, slot], to, p.core)

    def core_copy(self, turn, slot):
        p = self.place
        ref = self.weights[slot].at[self.order[turn], :, :, p.core]
        sems = self.core_sems
        return remote(ref, ref, sems.at[0, turn, slot], sems.at[1, turn, slot], p.client, 1 - p.core)

    def launch(self, copy):
        copy.start()
        self.copies.append(copy)

    def begin(self, master):
        p = self.place
        start = 0
        for slot in range(3):
            rows = self.weights[slot].shape[-2]
            self.weights[slot][p.z, p.y, p.x, p.core] = master[start : start + rows, :].astype(low_type)
            start += rows
        for slot in range(3):
            self.launch(self.near_copy(0, slot))
            for step in range(3):
                self.launch(self.z_copy(step, slot))

    def steps(self):
        listed = []
        for turn in range(6):
            for slot in range(3):
                if 1 <= turn < 4:
                    listed.append(functools.partial(self.near_step, turn, slot))
                if 1 <= turn < 5:
                    listed.append(functools.partial(self.far_step, turn - 1, slot))
                if 2 <= turn:
                    listed.append(functools.partial(self.core_step, turn - 2, slot))
        return listed

    def near_step(self, turn, slot):
        self.z_copy(turn - 1, slot).wait_recv()
        self.launch(self.near_copy(turn, slot))

    def far_step(self, turn, slot):
        self.near_copy(turn, slot).wait_recv()
        self.launch(self.far_copy(turn, slot))

    def core_step(self, turn, slot):
        self.far_copy(turn, slot).wait_recv()
        self.launch(self.core_copy(turn, slot))

    def arrive(self, slot):
        for turn in range(4):
            self.core_copy(turn, slot).wait_recv()

    def drain(self):
        for copy in self.copies:
            copy.wait_send()


def norm_stats(mine, theirs, count):
    gap = mine[0:1] - theirs[0:1]
    mean = 0.5 * (mine[0:1] + theirs[0:1])
    spread = mine[1:2] + theirs[1:2] + gap * gap * (0.5 * count)
    return mean, lax.rsqrt(spread / (2.0 * count) + norm_epsilon)


def client_kernel(
    gather,
    images,
    classes,
    features,
    labels,
    flag,
    params,
    head,
    *rest,
):
    if gather:
        master, *rest = rest
    else:
        first_in, middle_in, last_in, *rest = rest
    (
        grad_first_out,
        grad_middle_out,
        grad_last_out,
        grad_norm_out,
        grad_head_out,
        loss_out,
        x_all,
        mid_wide,
        w_first,
        w_middle,
        w_last,
        act_one,
        act_two,
        act_three,
        taps_one,
        taps_two,
        hidden_two,
        stage,
        outgoing,
        params_all,
        head_all,
        pool_acc,
        slope_acc,
        slope_normed_acc,
        grad_pool,
        pool_send,
        pool_all,
        logit_grads,
        sums_mine,
        sums_theirs,
        shift,
        fwd_stats,
        sem_local,
        sem_swap,
        sem_misc,
        *gather_sems,
    ) = rest
    place = Place()
    core = place.core
    mate = (place.client, 1 - core)
    count_rows, channels = x_all.shape
    half = channels // 2
    width = act_one.shape[1]
    part = width // 2
    mine_images = images // 2
    line = SIDE * mine_images
    total_rows = 2.0 * count_rows

    def tile(index):
        return pl.ds(pl.multiple_of(index * line, line), line)

    def lanes(index, size):
        return pl.ds(pl.multiple_of(index * size, size), size)

    place.greet(gather)

    own_rows = pl.ds(pl.multiple_of(core * count_rows, count_rows), count_rows)
    mate_rows = pl.ds(pl.multiple_of((1 - core) * count_rows, count_rows), count_rows)
    copy_own = pltpu.make_async_copy(features.at[own_rows, :], mid_wide.at[core], sem_local.at[0])
    copy_own.start()
    to_mate = [
        remote(params, params_all.at[core], sem_misc.at[0, 0], sem_misc.at[1, 0], *mate),
        remote(head, head_all.at[core], sem_misc.at[0, 1], sem_misc.at[1, 1], *mate),
        remote(features.at[mate_rows, :], mid_wide.at[core], sem_misc.at[0, 2], sem_misc.at[1, 2], *mate),
    ]
    for copy in to_mate:
        copy.start()
    params_all[core] = params[...]
    head_all[core] = head[...]

    weights = (w_first, w_middle, w_last)
    if gather:
        spread = Spread(place, weights, gather_sems)
        spread.begin(master)
    else:
        loads = [
            pltpu.make_async_copy(src, dst, sem_local.at[1 + slot])
            for slot, (src, dst) in enumerate(zip((first_in, middle_in, last_in), weights))
        ]
        for load in loads:
            load.start()

    taps_one[...] = jnp.zeros_like(taps_one)
    taps_two[...] = jnp.zeros_like(taps_two)

    copy_own.wait()
    for copy in to_mate:
        copy.wait_recv()

    def turn(index, carry):
        per_half = half // LANES
        stage[...] = mid_wide[index // per_half, :, lanes(index % per_half, LANES)].astype(wide)

        def pixel(spot, inner):
            x_all[
                pl.ds(pl.multiple_of(spot * mine_images, mine_images), mine_images),
                lanes(index, LANES),
            ] = stage[pl.ds(spot, mine_images, stride=PIXELS), :].astype(low_type)
            return inner

        return lax.fori_loop(0, PIXELS, pixel, carry, unroll=7)

    chunks = channels // LANES
    if gather:
        steps = spread.steps()
        for spot, step in enumerate(steps):
            step()
            lower, upper = spot * chunks // len(steps), (spot + 1) * chunks // len(steps)
            if upper > lower:
                lax.fori_loop(lower, upper, turn, 0)
        for slot in range(3):
            spread.arrive(slot)
    else:
        lax.fori_loop(0, chunks, turn, 0)
        for load in loads:
            load.wait()

    def swap(slot, size):
        return remote(
            sums_mine.at[slot, :, pl.ds(0, size)],
            sums_theirs.at[slot, :, pl.ds(0, size)],
            sem_swap.at[0, slot],
            sem_swap.at[1, slot],
            *mate,
        )

    def gain_bias(lower, upper):
        rows = []
        for kind in range(2):
            pieces = [params_all[side, kind : kind + 1, lower:upper] for side in range(2)]
            rows.append(jnp.concatenate(pieces, axis=1))
        return rows

    def collect(index, value, columns, size):
        @pl.when(index == 0)
        def _():
            shift[0:1, pl.ds(0, size)] = column_sum(fold_rows(value)) / value.shape[0]
            shift[8:24, pl.ds(0, size)] = jnp.zeros((16, size), wide)

        gap = value - shift[0:1, pl.ds(0, size)]
        shift[8:16, pl.ds(0, size)] += fold_rows(gap)
        shift[16:24, pl.ds(0, size)] += fold_rows(gap * gap)

    def close_stats(slot, columns, size):
        sum_gap = column_sum(shift[8:16, pl.ds(0, size)])
        sum_square = column_sum(shift[16:24, pl.ds(0, size)])
        sums_mine[slot, 0:1, columns] = shift[0:1, pl.ds(0, size)] + sum_gap / count_rows
        sums_mine[slot, 1:2, columns] = sum_square - sum_gap * sum_gap / count_rows

    def settle(slot, size):
        mean, scale = norm_stats(
            sums_mine[slot, 0:2, pl.ds(0, size)], sums_theirs[slot, 0:2, pl.ds(0, size)], float(count_rows)
        )
        fwd_stats[slot, 0:1, pl.ds(0, size)] = mean
        fwd_stats[slot, 1:2, pl.ds(0, size)] = scale

    whole_width = pl.ds(0, width)

    def first_tile(index, carry):
        value = dot_nn(x_all[tile(index), :], flat_rows(w_first[...]))
        act_one[tile(index), :] = value
        collect(index, value, whole_width, width)
        return carry

    lax.fori_loop(0, SIDE, first_tile, 0)
    close_stats(0, whole_width, width)
    move = swap(0, width)
    move.start()
    move.wait()
    settle(0, width)

    gain_one, bias_one = gain_bias(0, part)
    gain_two, bias_two = gain_bias(part, width)
    gain_three, bias_three = gain_bias(width, width + half)

    def spread_taps(buffer, index, value):
        base = pl.multiple_of((index + 1) * line, line)
        step = mine_images
        buffer[pl.ds(base, line), width : 2 * width] = value
        buffer[pl.ds(pl.multiple_of(base + step, step), line - step), 0:width] = value[: line - step]
        buffer[pl.ds(base, line - step), 2 * width : 3 * width] = value[step:]

    def normal(act, slot, index):
        mean = fwd_stats[slot, 0:1, pl.ds(0, width)]
        return (act[tile(index), :] - mean) * fwd_stats[slot, 1:2, pl.ds(0, width)]

    def hide_one(index, carry):
        value = normal(act_one, 0, index) * gain_one + bias_one
        spread_taps(taps_one, index, (value * sigmoid(value)).astype(low_type))
        return carry

    lax.fori_loop(0, SIDE, hide_one, 0)

    def shifted(buffer, index, down):
        return buffer[pl.ds(pl.multiple_of((index + down) * line, line), line), :]

    def second_tile(index, carry):
        kernel = flat_rows(w_middle[...])
        value = dot_nn(shifted(taps_one, index, 0), kernel[0 : 3 * width])
        value += dot_nn(shifted(taps_one, index, 1), kernel[3 * width : 6 * width])
        value += dot_nn(shifted(taps_one, index, 2), kernel[6 * width :])
        act_two[tile(index), :] = value
        collect(index, value, whole_width, width)
        return carry

    lax.fori_loop(0, SIDE, second_tile, 0)
    close_stats(1, whole_width, width)
    move_two = swap(1, width)
    move_two.start()
    move_two.wait()
    settle(1, width)

    def hide_two(index, carry):
        value = normal(act_two, 1, index) * gain_two + bias_two
        hidden_two[tile(index), :] = (value * sigmoid(value)).astype(low_type)
        return carry

    lax.fori_loop(0, SIDE, hide_two, 0)

    groups = w_last.shape[0]
    group = channels // groups

    def third_group(which, carry):
        columns = lanes(which, group)

        def third_tile(index, inner):
            value = dot_nt(hidden_two[tile(index), :], flat_rows(w_last[which]))
            act_three[tile(index), columns] = value
            collect(index, value, columns, group)
            return inner

        lax.fori_loop(0, SIDE, third_tile, 0)
        close_stats(2, columns, group)
        return carry

    lax.fori_loop(0, groups, third_group, 0)
    move_three = swap(2, channels)
    move_three.start()
    move_three.wait()
    settle(2, channels)
    fwd_stats[2, 2:3, :] = gain_three
    fwd_stats[2, 3:4, :] = bias_three

    per_half = half // LANES

    def block_of(spot):
        return pl.ds(pl.multiple_of(spot * mine_images, mine_images), mine_images)

    def emit(index, carry):
        columns = lanes(index, LANES)
        mean, scale = fwd_stats[2, 0:1, columns], fwd_stats[2, 1:2, columns]
        gain, bias = fwd_stats[2, 2:3, columns], fwd_stats[2, 3:4, columns]

        def pixel(spot, sums):
            pooled, slopes, slopes_normed = sums
            normed = (act_three[block_of(spot), columns] - mean) * scale
            total = normed * gain + bias + x_all[block_of(spot), columns].astype(wide)
            sig = sigmoid(total)
            out = total * sig
            slope = sig + out * (1.0 - sig)
            mid_wide[index // per_half, block_of(spot), lanes(index % per_half, LANES)] = slope.astype(low_type)
            return pooled + out, slopes + slope, slopes_normed + slope * normed

        zero = jnp.zeros((mine_images, LANES), wide)
        pooled, slopes, slopes_normed = lax.fori_loop(0, PIXELS, pixel, (zero, zero, zero), unroll=7)
        pool_acc[:, columns] = pooled
        slope_acc[:, columns] = slopes
        slope_normed_acc[:, columns] = slopes_normed
        return carry

    lax.fori_loop(0, channels // LANES, emit, 0)

    pooled = (pool_acc[...] / PIXELS).astype(low_type)
    head_full = flat_rows(head_all[...])
    logits = dot_nn(pooled, head_full)
    spots = lax.broadcasted_iota(jnp.int32, logits.shape, 1)
    inside = spots < classes
    onehot = (spots == labels[pl.ds(pl.multiple_of(core * mine_images, mine_images), mine_images), :]).astype(wide)
    top = jnp.max(jnp.where(inside, logits, -jnp.inf), axis=1, keepdims=True)
    powers = jnp.where(inside, jnp.exp(logits - top), 0.0)
    power_sum = jnp.sum(powers, axis=1, keepdims=True)
    picked = jnp.sum(logits * onehot, axis=1, keepdims=True)
    each_loss = top + jnp.log(power_sum) - picked
    taking = flag[0].astype(wide)
    loss_out[...] = jnp.full(loss_out.shape, taking * jnp.sum(each_loss), wide)
    grads = (taking / images * (powers / power_sum - onehot)).astype(low_type)
    grad_pool[...] = dot_nt(grads, head_full) / PIXELS
    logit_grads[core] = grads
    pool_all[core] = pooled[:, 0:half]
    pool_send[...] = pooled[:, half:]

    @pl.when(core == 1)
    def _():
        pool_all[core] = pooled[:, half:]
        pool_send[...] = pooled[:, 0:half]

    head_moves = [
        remote(pool_send, pool_all.at[core], sem_misc.at[0, 3], sem_misc.at[1, 3], *mate),
        remote(logit_grads.at[core], logit_grads.at[core], sem_misc.at[0, 4], sem_misc.at[1, 4], *mate),
    ]

    sums_mine[3, 0:1, :] = column_sum(grad_pool[...] * slope_acc[...])
    sums_mine[3, 1:2, :] = column_sum(grad_pool[...] * slope_normed_acc[...])
    move_back = swap(3, channels)
    move_back.start()
    for copy in head_moves:
        copy.start()
    move_back.wait()

    def back_terms(slot, layer, size, gain):
        columns = pl.ds(0, size)
        sums = sums_mine[slot, 0:2, columns] + sums_theirs[slot, 0:2, columns]
        sums_mine[slot, 2:4, columns] = sums
        scale = fwd_stats[layer, 1:2, columns]
        return (
            scale * gain,
            scale * gain * sums[0:1] / total_rows,
            scale * scale * gain * sums[1:2] / total_rows,
        )

    first, second, third = back_terms(3, 2, channels, gain_three)
    fwd_stats[2, 4:5, :] = first
    fwd_stats[2, 5:6, :] = second
    fwd_stats[2, 6:7, :] = third

    def pull(index, carry):
        columns = lanes(index, LANES)
        mean = fwd_stats[2, 0:1, columns]
        first, second = fwd_stats[2, 4:5, columns], fwd_stats[2, 5:6, columns]
        third = fwd_stats[2, 6:7, columns]
        reach = grad_pool[:, columns] * first

        def pixel(spot, inner):
            where = (index // per_half, block_of(spot), lanes(index % per_half, LANES))
            slope = mid_wide[where].astype(wide)
            gap = act_three[block_of(spot), columns] - mean
            mid_wide[where] = (reach * slope - second - third * gap).astype(low_type)
            return inner

        return lax.fori_loop(0, PIXELS, pixel, carry, unroll=7)

    lax.fori_loop(0, channels // LANES, pull, 0)
    for copy in head_moves:
        copy.wait_recv()
    grad_head_out[...] = dot_tn(flat_rows(pool_all[...]), flat_rows(logit_grads[...]))

    def drop_into(index, value, act, slot, gain, bias, columns):
        normed = normal(act, slot, index)
        norm = normed * gain + bias
        sig = sigmoid(norm)
        grad = value * (sig + norm * sig * (1.0 - sig))
        act_three[tile(index), columns] = grad
        size = pl.ds(0, width)

        @pl.when(index == 0)
        def _():
            shift[8:24, size] = jnp.zeros((16, width), wide)

        shift[8:16, size] += fold_rows(grad)
        shift[16:24, size] += fold_rows(grad * normed)

    def close_back(slot):
        size = pl.ds(0, width)
        sums_mine[slot, 0:1, size] = column_sum(shift[8:16, size])
        sums_mine[slot, 1:2, size] = column_sum(shift[16:24, size])

    space_two, space_one = pl.ds(0, width), pl.ds(width, width)

    def back_two(index, carry):
        kernel = flat_rows(w_last[...])
        value = dot_nn(mid_wide[0, tile(index), :], kernel[:half])
        value += dot_nn(mid_wide[1, tile(index), :], kernel[half:])
        drop_into(index, value, act_two, 1, gain_two, bias_two, space_two)
        return carry

    lax.fori_loop(0, SIDE, back_two, 0)
    close_back(4)
    move_back_two = swap(4, width)
    move_back_two.start()

    def put(out, block, value):
        slot = block % 2
        rows = lanes(block, group)

        @pl.when(block >= 2)
        def _():
            pltpu.make_async_copy(outgoing.at[slot], out.at[rows, :], sem_local.at[4 + slot]).wait()

        outgoing[slot] = value.astype(low_type)
        pltpu.make_async_copy(outgoing.at[slot], out.at[rows, :], sem_local.at[4 + slot]).start()

    def drain(out, blocks):
        for block in (blocks - 2, blocks - 1):
            slot = block % 2
            pltpu.make_async_copy(
                outgoing.at[slot], out.at[pl.ds(block * group, group), :], sem_local.at[4 + slot]
            ).wait()

    per_side = half // group

    def expand_block(block, carry):
        left = mid_wide[block // per_side, :, lanes(block % per_side, group)]
        put(grad_last_out, block, dot_tn(left, hidden_two[...]))
        return carry

    lax.fori_loop(0, channels // group, expand_block, 0)
    drain(grad_last_out, channels // group)
    move_back_two.wait()
    terms_two = back_terms(4, 1, width, gain_two)

    def back_act(terms, act, layer, index, columns):
        first, second, third = terms
        gap = act[tile(index), :] - fwd_stats[layer, 0:1, pl.ds(0, width)]
        return (first * act_three[tile(index), columns] - second - third * gap).astype(low_type)

    def grad_two(index, carry):
        spread_taps(taps_two, index, back_act(terms_two, act_two, 1, index, space_two))
        return carry

    lax.fori_loop(0, SIDE, grad_two, 0)

    def back_one(index, carry):
        kernel = flat_rows(w_middle[...])
        value = jnp.zeros((line, width), wide)
        for down in range(3):
            rows = shifted(taps_two, index, 2 - down)
            for over in range(3):
                tap = 3 * down + over
                value += dot_nt(
                    rows[:, (2 - over) * width : (3 - over) * width],
                    kernel[tap * width : (tap + 1) * width],
                )
        drop_into(index, value, act_one, 0, gain_one, bias_one, space_one)
        return carry

    lax.fori_loop(0, SIDE, back_one, 0)
    close_back(5)
    move_back_one = swap(5, width)
    move_back_one.start()

    def middle_block(block, carry):
        rows = pl.ds(pl.multiple_of((block // 3) * line, line), count_rows)
        left = taps_one[rows, lanes(block % 3, width)]
        put(grad_middle_out, block, dot_tn(left, taps_two[line : line + count_rows, width : 2 * width]))
        return carry

    lax.fori_loop(0, 9, middle_block, 0)
    drain(grad_middle_out, 9)
    move_back_one.wait()
    terms_one = back_terms(5, 0, width, gain_one)

    def grad_one(index, carry):
        hidden_two[tile(index), :] = back_act(terms_one, act_one, 0, index, space_one)
        return carry

    lax.fori_loop(0, SIDE, grad_one, 0)

    def reduce_block(block, carry):
        put(grad_first_out, block, dot_tn(x_all[:, lanes(block, group)], hidden_two[...]))
        return carry

    lax.fori_loop(0, channels // group, reduce_block, 0)

    for kind in range(2):
        row = 3 - kind
        grad_norm_out[kind : kind + 1, 0:part] = sums_mine[5, row : row + 1, lanes(core, part)]
        grad_norm_out[kind : kind + 1, part:width] = sums_mine[4, row : row + 1, lanes(core, part)]
        grad_norm_out[kind : kind + 1, width:] = sums_mine[3, row : row + 1, lanes(core, half)]

    drain(grad_first_out, channels // group)
    for copy in to_mate + head_moves:
        copy.wait_send()
    if gather:
        spread.drain()


def client_pass(gather, classes, features, labels, flag, params, head_low, weights):
    pixels, half = features.shape
    images = labels.shape[0]
    count_rows, channels = pixels // 2, 2 * half
    width = params.shape[1] - half
    classes_wide = LANES
    mine_images = images // 2
    line = SIDE * mine_images
    middle = 9 * width
    blocks = 32
    group = channels // SPOTS[0]
    any_space = pl.BlockSpec(memory_space=pl.ANY)
    vmem = pl.BlockSpec(memory_space=pltpu.VMEM)
    smem = pl.BlockSpec(memory_space=pltpu.SMEM)
    spots = SPOTS + (2,)
    scratch = [
        pltpu.VMEM((count_rows, channels), low_type),
        pltpu.VMEM((2, count_rows, half), low_type),
        pltpu.VMEM(spots + (channels // blocks, width), low_type),
        pltpu.VMEM(spots + (middle // blocks, width), low_type),
        pltpu.VMEM(spots + (channels // blocks, width), low_type),
        pltpu.VMEM((count_rows, width), wide),
        pltpu.VMEM((count_rows, width), wide),
        pltpu.VMEM((count_rows, channels), wide),
        pltpu.VMEM((count_rows + 2 * line, 3 * width), low_type),
        pltpu.VMEM((count_rows + 2 * line, 3 * width), low_type),
        pltpu.VMEM((count_rows, width), low_type),
        pltpu.VMEM((count_rows, LANES), wide),
        pltpu.VMEM((2, group, width), low_type),
        pltpu.VMEM((2,) + params.shape, wide),
        pltpu.VMEM((2, half, classes_wide), low_type),
        pltpu.VMEM((mine_images, channels), wide),
        pltpu.VMEM((mine_images, channels), wide),
        pltpu.VMEM((mine_images, channels), wide),
        pltpu.VMEM((mine_images, channels), wide),
        pltpu.VMEM((mine_images, half), low_type),
        pltpu.VMEM((2, mine_images, half), low_type),
        pltpu.VMEM((2, mine_images, classes_wide), low_type),
        pltpu.VMEM((6, 8, channels), wide),
        pltpu.VMEM((6, 8, channels), wide),
        pltpu.VMEM((24, max(width, group)), wide),
        pltpu.VMEM((3, 8, channels), wide),
        pltpu.SemaphoreType.DMA((6,)),
        pltpu.SemaphoreType.DMA((2, 6)),
        pltpu.SemaphoreType.DMA((2, 5)),
    ]
    if gather:
        scratch += [pltpu.SemaphoreType.DMA((2, 3, 3))]
        scratch += [pltpu.SemaphoreType.DMA((2, 4, 3)) for _ in range(3)]
    return pl.pallas_call(
        functools.partial(client_kernel, gather, images, classes),
        out_shape=(
            jax.ShapeDtypeStruct((channels, width), low_type),
            jax.ShapeDtypeStruct((middle, width), low_type),
            jax.ShapeDtypeStruct((channels, width), low_type),
            jax.ShapeDtypeStruct(params.shape, wide),
            jax.ShapeDtypeStruct((half, classes_wide), wide),
            jax.ShapeDtypeStruct((8, LANES), wide),
        ),
        in_specs=[any_space, vmem, smem, vmem, vmem] + ([vmem] if gather else [any_space] * 3),
        out_specs=(any_space, any_space, any_space, vmem, vmem, vmem),
        scratch_shapes=scratch,
        compiler_params=pltpu.CompilerParams(
            collective_id=0, has_side_effects=True, vmem_limit_bytes=VMEM_BYTES
        ),
    )(features, labels, flag, params, head_low, *weights)


def adam_update(param, grad, first, second, rate, decay):
    first = adam_first * first + (1.0 - adam_first) * grad
    second = adam_second * second + (1.0 - adam_second) * grad * grad
    first_hat = first / (1.0 - adam_first**STEP)
    second_hat = second / (1.0 - adam_second**STEP)
    return (
        param - rate * (first_hat / (jnp.sqrt(second_hat) + adam_epsilon) + decay * param),
        first,
        second,
    )


def gram_of(section):
    return lax.dot_general(section, section, (((0,), (0,)), ((), ())), precision=precise)


def square(gram):
    return jnp.dot(gram, gram, precision=precise)


def times_poly(left, mixed):
    return schulz_first * left + jnp.dot(left, mixed, precision=precise)


def schulz(sections):
    raw_grams = lax.psum(tuple(gram_of(section) for section in sections), ("client", "chan"))
    factors = [1.0 / (jnp.sqrt(jnp.trace(gram)) + 1e-07) for gram in raw_grams]
    current = [section * factor for section, factor in zip(sections, factors)]
    grams = [gram * (factor * factor) for gram, factor in zip(raw_grams, factors)]
    for turn in range(NS_STEPS):
        mixed = [schulz_second * gram + schulz_third * square(gram) for gram in grams]
        current = [times_poly(current[slot], mixed[slot]) for slot in range(3)]
        if turn + 1 < NS_STEPS:
            grams = [
                times_poly(times_poly(grams[slot], mixed[slot]), mixed[slot]) for slot in range(3)
            ]
    return current


def on_device(
    features,
    labels,
    mask,
    base_master,
    base_momentum,
    global_base,
    norm_params,
    norm_first,
    norm_second,
    head,
    head_first,
    head_second,
):
    halves = lax.axis_size("chan")
    blocks = lax.axis_size("client") * halves
    half = features.shape[2]
    width = base_master.shape[2]
    channels = half * halves
    images = labels.shape[1]
    classes = head.shape[2]
    rows_first = channels // blocks
    rows_mid = 9 * width // blocks
    bounds = (0, rows_first, rows_first + rows_mid, base_master.shape[1])
    master = base_master[0]
    head_low = jnp.pad(head[0].astype(low_type), ((0, 0), (0, LANES - classes)))
    low_master = master.astype(low_type)
    weights = [
        lax.all_gather(low_master[bounds[slot] : bounds[slot + 1]], ("client", "chan"), axis=0, tiled=True)
        for slot in range(3)
    ]
    weights = [weight.reshape(SPOTS + (2, weight.shape[0] // 32, width)) for weight in weights]
    grad_first, grad_middle, grad_last, grad_norm, grad_head, loss_tile = client_pass(
        False, classes, features[0], labels.reshape(images, 1), mask, norm_params[0, :, 0, :], head_low, weights
    )
    loss_sum, count = lax.psum(
        (loss_tile[0, 0], mask[0].astype(wide) * (images / halves)), ("client", "chan")
    )
    loss = jnp.stack([loss_sum, count])
    sums = [
        lax.psum_scatter(grad.astype(wide), ("client", "chan"), scatter_dimension=0, tiled=True)
        for grad in (grad_first, grad_middle, grad_last)
    ]
    grad_base = jnp.concatenate(sums, axis=0) + prox_weight * (master - global_base[0])
    momentum_new = momentum_decay * base_momentum[0] + grad_base
    current = schulz([momentum_new[bounds[slot] : bounds[slot + 1]] for slot in range(3)])
    ratio = (channels / width) ** 0.5
    ortho = jnp.concatenate([current[0] * ratio, current[1] * 3.0, current[2] * ratio], axis=0)
    base_new = master - muon_rate * (ortho + muon_decay * master)
    norm_new, norm_first_new, norm_second_new = adam_update(
        norm_params, grad_norm[None, :, None, :], norm_first, norm_second, norm_rate, 0.0
    )
    head_new, head_first_new, head_second_new = adam_update(
        head, grad_head[None, :, :classes], head_first, head_second, head_rate, head_decay
    )
    return (
        loss,
        base_new[None],
        momentum_new[None],
        base_new.astype(low_type)[None],
        norm_new,
        norm_first_new,
        norm_second_new,
        head_new,
        head_first_new,
        head_second_new,
    )


def solution(mesh):
    wide_block = P(("client", "chan"), None, None)
    norm_block = P("client", None, "chan", None)
    head_block = P("client", "chan", None)
    return jax.shard_map(
        on_device,
        mesh=mesh,
        in_specs=(P("client", None, "chan"), P("client", None), P("client"))
        + (wide_block,) * 3
        + (norm_block,) * 3
        + (head_block,) * 3,
        out_specs=(P(),) + (wide_block,) * 3 + (norm_block,) * 3 + (head_block,) * 3,
        check_vma=False,
    )
```

time: 1300 us -> 995 us (0.77)
  local copies, waits for them, and re-layouts: 426 us -> 13.8 us
  waiting for transfers between devices: 497 us -> 670 us
  Pallas kernels: 0 us -> 105 us
  matrix products: 198 us -> 112 us
  other arithmetic: 83.9 us -> 26.6 us
  blocking collectives: 68.3 us -> 40.6 us
    slice x16 -> x3, local copies, waits for them, and re-layouts: 226 us -> 2.52 us  [the longest x2 1.33 us: on_device(): low_master[bounds[slot]:bounds[slot + 1]]]
    reduce_scatter x5 -> x3, waiting for transfers between devices: 290 us -> 404 us  [on_device(): lax.psum_scatter(grad.astype(wide), ('client', 'chan'), scatter_dimension...]
    pallas_call x0 -> x1, Pallas kernels: none -> 105 us  [client_pass(): pl.pallas_call(functools.partial(client_kernel, gather, images, classes),...]
    reshape x4 -> x1, local copies, waits for them, and re-layouts: 101 us -> 1.36 us  [on_device(): labels.reshape(images, 1)]
    dot_general x11 -> x0, matrix products: 94.3 us -> none  [the longest x4 35.3 us: contract_rows(): lax.dot_general(left, right, (((0,), (0,)), ((), ())), preferred_element_...]
    all_gather x6 -> x3, waiting for transfers between devices: 121 us -> 179 us  [on_device(): lax.all_gather(low_master[bounds[slot]:bounds[slot + 1]], ('client', 'cha...]
    concatenate x9 -> x0, local copies, waits for them, and re-layouts: 48.4 us -> none  [patches_of(): return jnp.concatenate(taps, axis=-1).reshape(images * 49, 9 * width)]
    reduce_sum x12 -> x2, other arithmetic: 36.5 us -> 2.98 us  [schulz(): factors = [1.0 / (jnp.sqrt(jnp.trace(gram)) + 1e-07) for gram in raw_grams]]
  transfers between devices with their start and end apart: 12 -> 7, of which waited for: 10 -> 7; matrix products, arithmetic and copies ran while one was open for 12% -> 3% of each run, Pallas kernels for 0% -> 0%
where the time goes in v2:
time: 995 us; the launch traced here: 987 us
  waiting for transfers between devices  670 us (67%)
  matrix products  112 us (11%)
  Pallas kernels  105 us (11%)
  blocking collectives  40.6 us (4%)
  other arithmetic  26.6 us (3%)
  between operations  18.1 us (2%)
  local copies, waits for them, and re-layouts  13.8 us (1%)
    reduce_scatter x3, waiting for transfers between devices, on_device(): lax.psum_scatter(grad.astype(wide), ('client', 'chan'), scatter_dimension...  404 us
    all_gather x3, waiting for transfers between devices, on_device(): lax.all_gather(low_master[bounds[slot]:bounds[slot + 1]], ('client', 'cha...  179 us
    pallas_call x1, Pallas kernels, client_pass(): pl.pallas_call(functools.partial(client_kernel, gather, images, classes),...  105 us
    psum x1, waiting for transfers between devices, schulz(): lax.psum(tuple((gram_of(section) for section in sections)), ('client', 'c...  85.8 us
    dot_general x39, matrix products, times_poly(): return schulz_first * left + jnp.dot(left, mixed, precision=precise)  72.7 us
    psum x1, blocking collectives, on_device(): lax.psum((loss_tile[0, 0], mask[0].astype(wide) * (images / halves)), ('c...  40.6 us
    dot_general x15, matrix products, square(): return jnp.dot(gram, gram, precision=precise)  32.9 us
  transfers between devices with their start and end apart: 7, of which 7 were waited for; matrix products, arithmetic and copies ran while one was open for 3% of the time, Pallas kernels for 0%

profile of v2, /device:TPU:0, one launch (start us, length us, event | category | flops | bytes accessed | tf_op | source)
XLA Modules:
  0.0 986.6 jit_solution(15233247641234192922)
XLA Ops:
  15.9 54.7 %all-gather.11.cloned.1.call-done = bf16[1,2048,512]{2,1,0:T(8,128)(2,1)} async-done(((bf16[1,64,512]{2,1,0:T(8,128)(2,1)}), bf16[1,2048,512]{2,1,0:T(8,128)(2,1)}) %all-gather.11.cloned.1.call-update) | async-done | bytes 2097168 | tf_op jit(solution)/shard_map/all_gather | solution.py:833
  70.5 58.7 %all-gather.7.cloned.1.call-done = bf16[1,2048,512]{2,1,0:T(8,128)(2,1)} async-done(((bf16[1,64,512]{2,1,0:T(8,128)(2,1)}), bf16[1,2048,512]{2,1,0:T(8,128)(2,1)}) %all-gather.7.cloned.1.call-update) | async-done | bytes 2097168 | tf_op jit(solution)/shard_map/all_gather | solution.py:833
  129.2 66.0 %all-gather.9.cloned.1.call-done = bf16[1,4608,512]{2,1,0:T(8,128)(2,1)} async-done(((bf16[1,144,512]{2,1,0:T(8,128)(2,1)}), bf16[1,4608,512]{2,1,0:T(8,128)(2,1)}) %all-gather.9.cloned.1.call-update) | async-done | bytes 4718608 | tf_op jit(solution)/shard_map/all_gather | solution.py:833
  195.2 105.4 %shard_map.195 = (bf16[2048,512]{1,0:T(8,128)(2,1)}, bf16[4608,512]{1,0:T(8,128)(2,1)}, bf16[2048,512]{1,0:T(8,128)(2,1)}, f32[2,1536]{1,0:T(2,128)}, f32[1024,128]{1,0:T(8,128)}, /*index=5*/f32[8,128]{1,0:T(8,128)}) custom-call(bf16[3136,1024]{1,0:T(8,128)(2,1)} %bitcast.136, s32[64,1]{1,0:T(8,128)} %copy.23.labels, s32[1]{0:T(128)S(6)} %copy.53.flag, ...), custom_call_target="tpu_custom_call" | custom-call | tf_op jit(solution)/shard_map/pallas_call | solution.py:747
  300.7 4.1 convert_element_type.33
  304.9 4.2 convert_element_type.35
  309.2 7.4 convert_element_type.34
  316.9 127.9 %reduce-scatter.4.cloned.1.call-done = f32[64,512]{1,0:T(8,128)} async-done(((f32[2048,512]{1,0:T(8,128)}), f32[64,512]{1,0:T(8,128)}) %reduce-scatter.4.cloned.1.call-update) | async-done | bytes 131088 | tf_op jit(solution)/shard_map/reduce_scatter | solution.py:845
  444.8 139.1 %reduce-scatter.8.cloned.1.call-done = f32[64,512]{1,0:T(8,128)} async-done(((f32[2048,512]{1,0:T(8,128)}), f32[64,512]{1,0:T(8,128)}) %reduce-scatter.8.cloned.1.call-update) | async-done | bytes 131088 | tf_op jit(solution)/shard_map/reduce_scatter | solution.py:845
  583.9 137.0 %reduce-scatter.6.cloned.1.call-done = f32[144,512]{1,0:T(8,128)} async-done(((f32[4608,512]{1,0:T(8,128)}), f32[144,512]{1,0:T(8,128)}) %reduce-scatter.6.cloned.1.call-update) | async-done | bytes 294928 | tf_op jit(solution)/shard_map/reduce_scatter | solution.py:845
  722.3 2.0 fusion.47
  724.3 2.1 fusion.41
  726.4 2.0 fusion.50
  730.4 40.6 %all-reduce.1 = (f32[1]{0:T(128)}, f32[1]{0:T(128)}) all-reduce(f32[1]{0:T(128)S(6)} %mul.392, f32[1]{0:T(128)} %bitcast.6), channel_id=1, replica_groups=mesh['client'=16,'chan'=2] {'client','chan'}, use_global_device_ids=true, to_apply=%region_1.2 | all-reduce | flops 2 | bytes 16 | tf_op jit(solution)/shard_map/psum | solution.py:840
  772.9 2.2 multiply_subtract_fusion
  775.2 1.9 copy.35
  780.9 85.8 %all-reduce.5.cloned.1.call-done = (f32[512,512]{1,0:T(8,128)}, f32[512,512]{1,0:T(8,128)}, f32[512,512]{1,0:T(8,128)}) async-done(((f32[512,512]{1,0:T(8,128)}, f32[512,512]{1,0:T(8,128)}, f32[512,512]{1,0:T(8,128)}), (f32[512,512]{1,0:T(8,128)}, f32[512,512]{1,0:T(8,128)}, f32[512,512]{1,0:T(8,128)})) %all-reduce.5.cloned.1.call-update) | async-done | bytes 3145744 | tf_op jit(solution)/shard_map/psum | solution.py:791
  866.7 2.3 select_reduce_fusion
  869.7 3.9 fusion.4
  873.7 2.9 convolution_add_fusion.7
  876.5 2.5 convolution_add_fusion.33
  879.7 4.0 fusion.9
  883.8 4.4 convolution_add_fusion.15
  891.4 1.9 fusion.14
  895.1 10.6 %convolution_add_fusion.23 = f32[512,512]{1,0:T(8,128)S(1)} fusion(f32[512,512]{1,0:T(8,128)S(1)} %fusion.14, f32[512,512]{1,0:T(8,128)S(1)} %copy-done, f32[]{:T(128)S(6)} %mul.403), kind=kOutput, calls=%fused_computation.51 | convolution fusion | flops 1611661312 | bytes 3145732 | tf_op jit(solution)/shard_map/dot_general | solution.py:787
  905.8 1.9 convolution_add_fusion.6
  907.7 1.9 fusion.3
  909.5 1.8 convolution_add_fusion.5
  911.4 1.8 convolution_add_fusion.4
  914.0 1.9 fusion.2
  917.8 2.1 convolution_add_fusion.2
  920.6 1.9 fusion.1
  924.4 1.9 convolution_add_fusion
  927.0 1.9 fusion
  930.7 2.3 fusion.8
  933.1 1.9 convolution_add_fusion.13
  937.5 1.9 fusion.7
  941.3 1.8 convolution_add_fusion.10
  943.9 1.9 fusion.6
  945.8 2.0 convolution_add_fusion.9
  947.8 1.9 convolution_add_fusion.8
  950.4 1.9 fusion.5
  954.1 1.9 fusion.13
  956.0 1.8 convolution_add_fusion.21
  957.9 2.1 convolution_add_fusion.20
  960.7 1.9 fusion.12
  967.1 1.9 fusion.11
  973.8 1.9 fusion.10
  (101 shorter events, 50.9 us)
Async XLA Ops:
  7.2 63.4 %all-gather.11.cloned.1.call-start = ((), (), s32[]{:S(2)}) async-start(), calls=%async_computation.8 | async-start | bytes 2162688 | tf_op jit(solution)/shard_map/all_gather | solution.py:833
  9.0 120.2 %all-gather.7.cloned.1.call-start = ((), (), s32[]{:S(2)}) async-start(), calls=%async_computation.6 | async-start | bytes 2162688 | tf_op jit(solution)/shard_map/all_gather | solution.py:833
  9.8 185.5 %all-gather.9.cloned.1.call-start = ((), (), s32[]{:S(2)}) async-start(), calls=%async_computation.7 | async-start | bytes 4866048 | tf_op jit(solution)/shard_map/all_gather | solution.py:833
  10.5 434.3 %reduce-scatter.4.cloned.1.call-start = ((), (), s32[]{:S(2)}) async-start(), calls=%async_computation.3 | async-start | bytes 4325376 | tf_op jit(solution)/shard_map/reduce_scatter | solution.py:845
  304.8 279.1 %reduce-scatter.8.cloned.1.call-start = ((), (), s32[]{:S(2)}) async-start(), calls=%async_computation.5 | async-start | bytes 4325376 | tf_op jit(solution)/shard_map/reduce_scatter | solution.py:845
  309.1 411.8 %reduce-scatter.6.cloned.1.call-start = ((), (), s32[]{:S(2)}) async-start(), calls=%async_computation.4 | async-start | bytes 9732096 | tf_op jit(solution)/shard_map/reduce_scatter | solution.py:845
  316.6 404.4 %copy-start.3 = (f32[1,272,512]{2,1,0:T(8,128)S(1)}, f32[1,272,512]{2,1,0:T(8,128)}, u32[]{:S(2)}) copy-start(f32[1,272,512]{2,1,0:T(8,128)} %param.15) | copy-start | bytes 1671172
  316.6 404.4 %copy-start.7 = (f32[1,272,512]{2,1,0:T(8,128)S(1)}, f32[1,272,512]{2,1,0:T(8,128)}, u32[]{:S(2)}) copy-start(f32[1,272,512]{2,1,0:T(8,128)} %param.16) | copy-start | bytes 1671172
  316.6 404.4 %copy-start.9 = (f32[1,272,512]{2,1,0:T(8,128)S(1)}, f32[1,272,512]{2,1,0:T(8,128)}, u32[]{:S(2)}) copy-start(f32[1,272,512]{2,1,0:T(8,128)} %param.17) | copy-start | bytes 1671172
  316.6 411.8 %copy-start.15 = (f32[1,1024,100]{1,0,2:T(1,128)S(1)}, f32[1,1024,100]{1,0,2:T(1,128)}, u32[]{:S(2)}) copy-start(f32[1,1024,100]{1,0,2:T(1,128)} %param.22) | copy-start | bytes 1228804
  316.6 550.1 %all-reduce.5.cloned.1.call-start = ((), (), s32[]{:S(2)}) async-start(), calls=%async_computation.9 | async-start | bytes 6291456 | tf_op jit(solution)/shard_map/psum | solution.py:791
  722.2 4.2 copy-start.2
  722.3 6.6 copy-start.16
  722.3 48.7 %copy-start.17 = (f32[1,2,1,1536]{3,2,1,0:T(1,128)S(1)}, f32[1,2,1,1536]{3,2,1,0:T(1,128)}, u32[]{:S(2)}) copy-start(f32[1,2,1,1536]{3,2,1,0:T(1,128)} %param.18) | copy-start | bytes 36868
  722.3 48.7 %copy-start.18 = (f32[1,2,1,1536]{3,2,1,0:T(1,128)S(1)}, f32[1,2,1,1536]{3,2,1,0:T(1,128)}, u32[]{:S(2)}) copy-start(f32[1,2,1,1536]{3,2,1,0:T(1,128)} %param.19) | copy-start | bytes 36868
  722.3 48.7 %copy-start.19 = (f32[1,2,1,1536]{3,2,1,0:T(1,128)S(1)}, f32[1,2,1,1536]{3,2,1,0:T(1,128)}, u32[]{:S(2)}) copy-start(f32[1,2,1,1536]{3,2,1,0:T(1,128)} %param.20) | copy-start | bytes 36868
  722.3 48.7 %copy-start.20 = (f32[2,1536]{1,0:T(2,128)S(1)}, f32[2,1536]{1,0:T(2,128)}, u32[]{:S(2)}) copy-start(f32[2,1536]{1,0:T(2,128)} %get-tuple-element.20) | copy-start | bytes 36868
  866.7 7.0 copy-start.1
  876.5 13.5 %copy-start = (f32[512,512]{1,0:T(8,128)S(1)}, f32[512,512]{1,0:T(8,128)}, u32[]{:S(2)}) copy-start(f32[512,512]{1,0:T(8,128)} %get-tuple-element.36) | copy-start | bytes 3145732
  891.4 14.3 %copy-start.6 = (f32[512,512]{1,0:T(8,128)S(1)}, f32[512,512]{1,0:T(8,128)}, u32[]{:S(2)}) copy-start(f32[512,512]{1,0:T(8,128)} %convolution_add_fusion.7) | copy-start | bytes 3145732
  907.6 5.6 copy-start.14
  924.4 4.5 copy-start.5
  972.7 5.2 copy-start.4
  972.7 5.2 copy-start.8
  972.7 5.2 copy-start.10
  972.7 5.2 copy-start.11
  972.7 5.2 copy-start.12
  972.7 5.2 copy-start.13
Sparse Core Ops, SparseCore 0:
  11.4 59.0 all-gather.10
  74.0 55.2 all-gather.6
  132.7 62.4 all-gather.8
  305.0 139.8 reduce-scatter.3
  447.0 136.9 reduce-scatter.7
  589.7 131.2 reduce-scatter.5
  728.5 138.1 all-reduce.4

commit v3 on v2

--- a/solution.py
+++ b/solution.py
@@ -503,7 +503,8 @@
     picked = jnp.sum(logits * onehot, axis=1, keepdims=True)
     each_loss = top + jnp.log(power_sum) - picked
     taking = flag[0].astype(wide)
-    loss_out[...] = jnp.full(loss_out.shape, taking * jnp.sum(each_loss), wide)
+    tile_spots = lax.broadcasted_iota(jnp.int32, loss_out.shape, 1)
+    loss_out[...] = jnp.where(tile_spots == 0, taking * jnp.sum(each_loss), taking * mine_images)
     grads = (taking / images * (powers / power_sum - onehot)).astype(low_type)
     grad_pool[...] = dot_nt(grads, head_full) / PIXELS
     logit_grads[core] = grads
@@ -763,6 +764,469 @@
     )(features, labels, flag, params, head_low, *weights)
 
 
+class Fold:
+    def __init__(self, place, sources, sums, boxes, sems):
+        self.place = place
+        self.sources = sources
+        self.sums = sums
+        self.core_boxes, self.near_boxes, self.far_boxes, self.z_boxes = boxes
+        self.core_sems, self.near_sems, self.far_sems, self.z_sems = sems
+        self.order = place.others[::-1] + [place.z]
+        self.copies = []
+
+    def core_copy(self, turn, slot):
+        p = self.place
+        sems = self.core_sems
+        return remote(
+            self.sources[slot].at[self.order[turn], :, :, 1 - p.core],
+            self.core_boxes[slot].at[turn],
+            sems.at[0, turn, slot],
+            sems.at[1, turn, slot],
+            p.client,
+            1 - p.core,
+        )
+
+    def near_copy(self, turn, slot):
+        p = self.place
+        spot = self.order[turn]
+        if slot == 1:
+            ref, to = self.sums[slot].at[spot, 1 - p.y], p.along_y()
+        else:
+            ref, to = self.sums[slot].at[spot, :, 1 - p.x], p.along_x()
+        sems = self.near_sems
+        return remote(
+            ref, self.near_boxes[slot].at[turn], sems.at[0, turn, slot], sems.at[1, turn, slot], to, p.core
+        )
+
+    def far_copy(self, turn, slot):
+        p = self.place
+        spot = self.order[turn]
+        if slot == 1:
+            ref, to = self.sums[slot].at[spot, p.y, 1 - p.x], p.along_x()
+        else:
+            ref, to = self.sums[slot].at[spot, 1 - p.y, p.x], p.along_y()
+        sems = self.far_sems
+        return remote(
+            ref, self.far_boxes[slot].at[turn], sems.at[0, turn, slot], sems.at[1, turn, slot], to, p.core
+        )
+
+    def z_copy(self, turn, slot):
+        p = self.place
+        step = 2 - turn
+        sems = self.z_sems
+        return remote(
+            self.sums[slot].at[self.order[turn], p.y, p.x],
+            self.z_boxes[slot].at[step],
+            sems.at[0, step, slot],
+            sems.at[1, step, slot],
+            p.along_z(step),
+            p.core,
+        )
+
+    def launch(self, copy):
+        copy.start()
+        self.copies.append(copy)
+
+    def core_step(self, turn, slot):
+        spot = self.order[turn]
+        self.core_copy(turn, slot).wait_recv()
+        both = self.local[slot][spot].astype(wide)
+        both += self.core_boxes[slot][turn].astype(wide)
+        self.sums[slot][spot] = both.astype(low_type)
+        self.launch(self.near_copy(turn, slot))
+
+    def near_step(self, turn, slot):
+        p = self.place
+        spot = self.order[turn]
+        self.near_copy(turn, slot).wait_recv()
+        where = (spot, p.y) if slot == 1 else (spot, slice(None), p.x)
+        both = self.sums[slot][where].astype(wide) + self.near_boxes[slot][turn].astype(wide)
+        self.sums[slot][where] = both.astype(low_type)
+        self.launch(self.far_copy(turn, slot))
+
+    def far_step(self, turn, slot):
+        p = self.place
+        where = (self.order[turn], p.y, p.x)
+        self.far_copy(turn, slot).wait_recv()
+        both = self.sums[slot][where].astype(wide) + self.far_boxes[slot][turn].astype(wide)
+        self.sums[slot][where] = both.astype(low_type)
+        if turn < 3:
+            self.launch(self.z_copy(turn, slot))
+
+    def begin(self, slot):
+        for turn in range(4):
+            self.launch(self.core_copy(turn, slot))
+
+    def steps(self):
+        listed = []
+        for turn in range(6):
+            for slot in range(3):
+                if turn < 4:
+                    listed.append(functools.partial(self.core_step, turn, slot))
+                if 1 <= turn < 5:
+                    listed.append(functools.partial(self.near_step, turn - 1, slot))
+                if 2 <= turn:
+                    listed.append(functools.partial(self.far_step, turn - 2, slot))
+        return listed
+
+    def result(self, slot):
+        p = self.place
+        total = self.sums[slot][p.z, p.y, p.x].astype(wide)
+        for step in range(3):
+            self.z_copy(2 - step, slot).wait_recv()
+            total += self.z_boxes[slot][step].astype(wide)
+        return total
+
+    def drain(self):
+        for copy in self.copies:
+            copy.wait_send()
+
+
+class GramSum:
+    def __init__(self, place, data, total, boxes, sems):
+        self.place = place
+        self.data = data
+        self.total = total
+        self.core_box, self.near_box, self.far_box, self.z_box = boxes
+        self.sems = sems
+        self.copies = []
+        self.sizes = (data.shape[0] // 72 * 40 // 32, data.shape[0] // 72 * 32 // 32)
+
+    def rows(self, kind, core, z=None, first=None, second=None):
+        size = self.sizes[kind]
+        start = core * (16 * (self.sizes[0] + self.sizes[1])) + kind * 16 * self.sizes[0]
+        count = 16 * size
+        for number, spot, parts in ((4 * size, z, 4), (2 * size, first, 2), (size, second, 2)):
+            if spot is None:
+                break
+            start, count = start + spot * number, number
+        return pl.ds(pl.multiple_of(start, 8), count)
+
+    def ways(self, kind):
+        p = self.place
+        x_way, y_way = (p.x, p.along_x()), (p.y, p.along_y())
+        return (x_way, y_way) if kind == 0 else (y_way, x_way)
+
+    def copy(self, phase, kind, turn, src, dst, client, core):
+        sems = self.sems
+        return remote(
+            src, dst, sems.at[0, phase, kind, turn], sems.at[1, phase, kind, turn], client, core
+        )
+
+    def launch(self, copy):
+        copy.start()
+        self.copies.append(copy)
+
+    def down(self, phase, kind, turn):
+        p = self.place
+        z = (p.others[::-1] + [p.z])[turn]
+        (first, first_to), (second, second_to) = self.ways(kind)
+        base = self.sizes[0] * kind
+        if phase == 0:
+            src = self.data.at[self.rows(kind, 1 - p.core, z), :]
+            box = self.core_box.at[turn, pl.ds(4 * base, 4 * self.sizes[kind]), :]
+            return self.copy(0, kind, turn, src, box, p.client, 1 - p.core)
+        if phase == 1:
+            src = self.data.at[self.rows(kind, p.core, z, 1 - first), :]
+            box = self.near_box.at[turn, pl.ds(2 * base, 2 * self.sizes[kind]), :]
+            return self.copy(1, kind, turn, src, box, first_to, p.core)
+        if phase == 2:
+            src = self.data.at[self.rows(kind, p.core, z, first, 1 - second), :]
+            box = self.far_box.at[turn, pl.ds(base, self.sizes[kind]), :]
+            return self.copy(2, kind, turn, src, box, second_to, p.core)
+        src = self.data.at[self.rows(kind, p.core, z, first, second), :]
+        box = self.z_box.at[turn, pl.ds(base, self.sizes[kind]), :]
+        return self.copy(3, kind, turn, src, box, p.along_z(2 - turn), p.core)
+
+    def down_step(self, phase, kind, turn):
+        p = self.place
+        z = (p.others[::-1] + [p.z])[turn]
+        (first, _), (second, _) = self.ways(kind)
+        self.down(phase, kind, turn).wait_recv()
+        spots = (z, first, second)[: phase + 1]
+        where = self.rows(kind, p.core, *spots)
+        scale = (4, 2, 1)[phase]
+        box = (self.core_box, self.near_box, self.far_box)[phase]
+        self.data[where, :] += box[turn, pl.ds(scale * self.sizes[0] * kind, scale * self.sizes[kind]), :]
+        if phase < 2 or turn < 3:
+            self.launch(self.down(phase + 1, kind, turn))
+
+    def up(self, phase, kind, turn):
+        p = self.place
+        z = ([p.z] + p.others)[turn]
+        (first, first_to), (second, second_to) = self.ways(kind)
+        if phase == 0:
+            ref, to = self.total.at[self.rows(kind, p.core, p.z, first, second), :], p.along_z(turn)
+        elif phase == 1:
+            ref, to = self.total.at[self.rows(kind, p.core, z, first, second), :], second_to
+        elif phase == 2:
+            ref, to = self.total.at[self.rows(kind, p.core, z, first), :], first_to
+        else:
+            ref, to = self.total.at[self.rows(kind, p.core, z), :], p.client
+        return self.copy(4 + phase, kind, turn, ref, ref, to, 1 - p.core if phase == 3 else p.core)
+
+    def run(self):
+        kinds = (0, 1)
+        for turn in range(4):
+            for kind in kinds:
+                self.launch(self.down(0, kind, turn))
+        for turn in range(6):
+            for kind in kinds:
+                for phase in range(3):
+                    if 0 <= turn - phase < 4:
+                        self.down_step(phase, kind, turn - phase)
+        p = self.place
+        for kind in kinds:
+            (first, _), (second, _) = self.ways(kind)
+            where = self.rows(kind, p.core, p.z, first, second)
+            value = self.data[where, :]
+            for turn in range(3):
+                self.down(3, kind, turn).wait_recv()
+                value += self.z_box[turn, pl.ds(self.sizes[0] * kind, self.sizes[kind]), :]
+            self.total[where, :] = value
+            self.launch(self.up(1, kind, 0))
+            for turn in range(3):
+                self.launch(self.up(0, kind, turn))
+        for turn in range(6):
+            for kind in kinds:
+                if 1 <= turn < 4:
+                    self.up(0, kind, turn - 1).wait_recv()
+                    self.launch(self.up(1, kind, turn))
+                if 1 <= turn < 5:
+                    self.up(1, kind, turn - 1).wait_recv()
+                    self.launch(self.up(2, kind, turn - 1))
+                if 2 <= turn:
+                    self.up(2, kind, turn - 2).wait_recv()
+                    self.launch(self.up(3, kind, turn - 2))
+        for turn in range(4):
+            for kind in kinds:
+                self.up(3, kind, turn).wait_recv()
+
+    def drain(self):
+        for copy in self.copies:
+            copy.wait_send()
+
+
+class TileSum:
+    def __init__(self, place, tiles, boxes, sems):
+        self.place = place
+        self.tiles = tiles
+        self.boxes = boxes
+        self.sems = sems
+
+    def copy(self, stage, box):
+        p = self.place
+        to = (p.client, p.along_x(), p.along_y()) + tuple(p.along_z(step) for step in range(3))
+        core = 1 - p.core if box == 0 else p.core
+        return remote(
+            self.tiles.at[stage], self.boxes.at[box], self.sems.at[0, box], self.sems.at[1, box], to[box], core
+        )
+
+    def steps(self):
+        def start():
+            self.copy(0, 0).start()
+
+        def pair(stage):
+            self.copy(stage, stage).wait_recv()
+            self.tiles[stage + 1] = self.tiles[stage] + self.boxes[stage]
+            if stage < 2:
+                self.copy(stage + 1, stage + 1).start()
+            else:
+                for step in range(3):
+                    self.copy(3, 3 + step).start()
+
+        return [start] + [functools.partial(pair, stage) for stage in range(3)]
+
+    def result(self):
+        for step in range(3):
+            self.copy(3, 3 + step).wait_recv()
+        return (self.tiles[3] + self.boxes[3]) + (self.boxes[4] + self.boxes[5])
+
+    def drain(self):
+        for stage in range(3):
+            self.copy(stage, stage).wait_send()
+        for step in range(3):
+            self.copy(3, 3 + step).wait_send()
+
+
+def dot_high(left, right):
+    return jnp.dot(left, right, precision=lax.Precision.HIGH, preferred_element_type=wide)
+
+
+def base_kernel(
+    ratios,
+    master,
+    momentum,
+    anchor,
+    loss_in,
+    first_in,
+    middle_in,
+    last_in,
+    base_new,
+    momentum_new,
+    base_low,
+    loss_out,
+    *rest,
+):
+    place = Place()
+    rest = list(rest)
+
+    def take(count):
+        taken = rest[:count]
+        del rest[:count]
+        return taken
+
+    sources, sums = take(3), take(3)
+    fold_boxes = [take(3) for _ in range(4)]
+    gram, gram_total = take(2)
+    gram_boxes = take(4)
+    grams, iterate, tiles, tile_boxes = take(4)
+    (local_sems,) = take(1)
+    fold_sems = take(4)
+    gram_sems, tile_sems = take(2)
+
+    place.greet(True)
+    incoming = (first_in, middle_in, last_in)
+    fold = Fold(place, incoming, sums, fold_boxes, fold_sems)
+    for slot in (2, 1, 0):
+        fold.begin(slot)
+    loads = [
+        pltpu.make_async_copy(incoming[slot].at[:, :, :, place.core], sources[slot], local_sems.at[slot])
+        for slot in range(3)
+    ]
+    for load in loads:
+        load.start()
+    tiles[0] = loss_in[...]
+    tile_sum = TileSum(place, tiles, tile_boxes, tile_sems)
+    extra = tile_sum.steps()
+    extra.pop(0)()
+    for load in loads:
+        load.wait()
+    fold.local = sources
+    steps = fold.steps()
+    for spot, step in enumerate(steps):
+        step()
+        if extra and spot % 9 == 8:
+            extra.pop(0)()
+    for step in extra:
+        step()
+
+    bounds = [0]
+    for slot in range(3):
+        bounds.append(bounds[-1] + sums[slot].shape[-2])
+    width = master.shape[1]
+    part = width // 2
+    for slot in range(3):
+        rows = slice(bounds[slot], bounds[slot + 1])
+        grad = fold.result(slot) + prox_weight * (master[rows, :] - anchor[rows, :])
+        fresh = momentum_decay * momentum[rows, :] + grad
+        momentum_new[rows, :] = fresh
+        partial = lax.dot_general(
+            fresh, fresh, (((0,), (0,)), ((), ())), precision=precise, preferred_element_type=wide
+        )
+        start = 3 * part * slot
+        gram[start : start + part, :] = partial[:part, :part]
+        gram[start + part : start + 2 * part, :] = partial[:part, part:]
+        gram[start + 2 * part : start + 3 * part, :] = partial[part:, part:]
+    loss_out[...] = tile_sum.result()
+
+    gram_sum = GramSum(place, gram, gram_total, gram_boxes, gram_sems)
+    gram_sum.run()
+
+    spots = lax.broadcasted_iota(jnp.int32, (part, part), 0)
+    diagonal = spots == lax.broadcasted_iota(jnp.int32, (part, part), 1)
+    iterate[...] = jnp.zeros_like(iterate)
+    for slot in range(3):
+        start = 3 * part * slot
+        corner = gram_total[start : start + part, :]
+        side = gram_total[start + part : start + 2 * part, :]
+        end = gram_total[start + 2 * part : start + 3 * part, :]
+        trace = jnp.sum(jnp.where(diagonal, corner + end, 0.0))
+        factor = 1.0 / (jnp.sqrt(trace) + 1e-07)
+        square = factor * factor
+        grams[slot, :part, :part] = corner * square
+        grams[slot, :part, part:] = side * square
+        grams[slot, part:, :part] = side.T * square
+        grams[slot, part:, part:] = end * square
+        rows = slice(bounds[slot], bounds[slot + 1])
+        iterate[slot, : bounds[slot + 1] - bounds[slot], :] = momentum_new[rows, :] * factor
+
+    def turn(slot, last):
+        current = grams[slot]
+        mixed = schulz_second * current + schulz_third * dot_high(current, current)
+        held = iterate[slot]
+        iterate[slot] = schulz_first * held + dot_high(held, mixed)
+        if not last:
+            once = schulz_first * current + dot_high(current, mixed)
+            grams[slot] = schulz_first * once + dot_high(once, mixed)
+
+    def one(count, carry):
+        turn(lax.rem(count, 3), False)
+        return carry
+
+    lax.fori_loop(0, 3 * (NS_STEPS - 1), one, 0)
+
+    def final(slot, carry):
+        turn(slot, True)
+        return carry
+
+    lax.fori_loop(0, 3, final, 0)
+    for slot in range(3):
+        rows = slice(bounds[slot], bounds[slot + 1])
+        held = master[rows, :]
+        ortho = iterate[slot, : bounds[slot + 1] - bounds[slot], :] * ratios[slot]
+        fresh = held - muon_rate * (ortho + muon_decay * held)
+        base_new[rows, :] = fresh
+        base_low[rows, :] = fresh.astype(low_type)
+    fold.drain()
+    gram_sum.drain()
+    tile_sum.drain()
+
+
+def base_pass(ratios, master, momentum, anchor, loss_tile, grads):
+    rows, width = master.shape
+    part = width // 2
+    any_space = pl.BlockSpec(memory_space=pl.ANY)
+    vmem = pl.BlockSpec(memory_space=pltpu.VMEM)
+    sizes = [grad.shape[0] // 32 for grad in grads]
+    grads = [grad.reshape(SPOTS + (2, size, width)) for grad, size in zip(grads, sizes)]
+    shares = [4, 4, 4, 3]
+
+    def boxes(lead):
+        return [pltpu.VMEM(lead + (size, width), low_type) for size in sizes]
+
+    scratch = boxes(SPOTS) + boxes(SPOTS)
+    scratch += boxes(SPOTS) + boxes((4, 2)) + boxes((4,)) + boxes((3,))
+    scratch += [pltpu.VMEM((9 * part, part), wide)] * 2
+    share = 9 * part // 32
+    scratch += [pltpu.VMEM((4, size, part), wide) for size in (4 * share, 2 * share, share)]
+    scratch += [pltpu.VMEM((3, share, part), wide)]
+    scratch += [
+        pltpu.VMEM((3, width, width), wide),
+        pltpu.VMEM((3, max(sizes), width), wide),
+        pltpu.VMEM((4, 8, LANES), wide),
+        pltpu.VMEM((6, 8, LANES), wide),
+        pltpu.SemaphoreType.DMA((3,)),
+    ]
+    scratch += [pltpu.SemaphoreType.DMA((2, 4, 3))] * 3 + [pltpu.SemaphoreType.DMA((2, 3, 3))]
+    scratch += [pltpu.SemaphoreType.DMA((2, 8, 2, 4)), pltpu.SemaphoreType.DMA((2, 6))]
+    return pl.pallas_call(
+        functools.partial(base_kernel, ratios),
+        out_shape=(
+            jax.ShapeDtypeStruct((rows, width), wide),
+            jax.ShapeDtypeStruct((rows, width), wide),
+            jax.ShapeDtypeStruct((rows, width), low_type),
+            jax.ShapeDtypeStruct((8, LANES), wide),
+        ),
+        in_specs=[vmem] * 4 + [any_space] * 3,
+        out_specs=(vmem,) * 4,
+        scratch_shapes=scratch,
+        compiler_params=pltpu.CompilerParams(
+            collective_id=1, has_side_effects=True, vmem_limit_bytes=VMEM_BYTES
+        ),
+    )(master, momentum, anchor, loss_tile, *grads)
+
+
 def adam_update(param, grad, first, second, rate, decay):
     first = adam_first * first + (1.0 - adam_first) * grad
     second = adam_second * second + (1.0 - adam_second) * grad * grad
@@ -800,6 +1264,19 @@
                 times_poly(times_poly(grams[slot], mixed[slot]), mixed[slot]) for slot in range(3)
             ]
     return current
+
+
+def base_far(ratios, bounds, master, momentum, anchor, loss_tile, grads):
+    sums = [
+        lax.psum_scatter(grad.astype(wide), ("client", "chan"), scatter_dimension=0, tiled=True)
+        for grad in grads
+    ]
+    grad_base = jnp.concatenate(sums, axis=0) + prox_weight * (master - anchor)
+    momentum_new = momentum_decay * momentum + grad_base
+    current = schulz([momentum_new[bounds[slot] : bounds[slot + 1]] for slot in range(3)])
+    ortho = jnp.concatenate([current[slot] * ratios[slot] for slot in range(3)], axis=0)
+    base_new = master - muon_rate * (ortho + muon_decay * master)
+    return base_new, momentum_new, base_new.astype(low_type), lax.psum(loss_tile, ("client", "chan"))
 
 
 def on_device(
@@ -828,29 +1305,35 @@
     bounds = (0, rows_first, rows_first + rows_mid, base_master.shape[1])
     master = base_master[0]
     head_low = jnp.pad(head[0].astype(low_type), ((0, 0), (0, LANES - classes)))
-    low_master = master.astype(low_type)
-    weights = [
-        lax.all_gather(low_master[bounds[slot] : bounds[slot + 1]], ("client", "chan"), axis=0, tiled=True)
-        for slot in range(3)
-    ]
-    weights = [weight.reshape(SPOTS + (2, weight.shape[0] // 32, width)) for weight in weights]
+    near = lax.axis_size("client") == SPOTS[0] * SPOTS[1] * SPOTS[2]
+    if near:
+        weights = [master]
+    else:
+        low_master = master.astype(low_type)
+        weights = [
+            lax.all_gather(low_master[bounds[slot] : bounds[slot + 1]], ("client", "chan"), axis=0, tiled=True)
+            for slot in range(3)
+        ]
+        weights = [weight.reshape(SPOTS + (2, weight.shape[0] // 32, width)) for weight in weights]
     grad_first, grad_middle, grad_last, grad_norm, grad_head, loss_tile = client_pass(
-        False, classes, features[0], labels.reshape(images, 1), mask, norm_params[0, :, 0, :], head_low, weights
+        near, classes, features[0], labels.reshape(images, 1), mask, norm_params[0, :, 0, :], head_low, weights
     )
-    loss_sum, count = lax.psum(
-        (loss_tile[0, 0], mask[0].astype(wide) * (images / halves)), ("client", "chan")
-    )
-    loss = jnp.stack([loss_sum, count])
-    sums = [
-        lax.psum_scatter(grad.astype(wide), ("client", "chan"), scatter_dimension=0, tiled=True)
-        for grad in (grad_first, grad_middle, grad_last)
-    ]
-    grad_base = jnp.concatenate(sums, axis=0) + prox_weight * (master - global_base[0])
-    momentum_new = momentum_decay * base_momentum[0] + grad_base
-    current = schulz([momentum_new[bounds[slot] : bounds[slot + 1]] for slot in range(3)])
     ratio = (channels / width) ** 0.5
-    ortho = jnp.concatenate([current[0] * ratio, current[1] * 3.0, current[2] * ratio], axis=0)
-    base_new = master - muon_rate * (ortho + muon_decay * master)
+    ratios = (ratio, 3.0, ratio)
+    if near:
+        base_new, momentum_new, base_low, loss_tile = base_pass(
+            ratios, master, base_momentum[0], global_base[0], loss_tile, (grad_first, grad_middle, grad_last)
+        )
+    else:
+        base_new, momentum_new, base_low, loss_tile = base_far(
+            ratios,
+            bounds,
+            master,
+            base_momentum[0],
+            global_base[0],
+            loss_tile,
+            (grad_first, grad_middle, grad_last),
+        )
     norm_new, norm_first_new, norm_second_new = adam_update(
         norm_params, grad_norm[None, :, None, :], norm_first, norm_second, norm_rate, 0.0
     )
@@ -858,10 +1341,10 @@
         head, grad_head[None, :, :classes], head_first, head_second, head_rate, head_decay
     )
     return (
-        loss,
+        loss_tile[0, 0:2],
         base_new[None],
         momentum_new[None],
-        base_new.astype(low_type)[None],
+        base_low[None],
         norm_new,
         norm_first_new,
         norm_second_new,

time: 995 us -> 304 us (0.31)
  waiting for transfers between devices: 670 us -> 0 us
  Pallas kernels: 105 us -> 283 us
  matrix products: 112 us -> 0 us
  blocking collectives: 40.6 us -> 0 us
  other arithmetic: 26.6 us -> 2.34 us
  between operations: 18.1 us -> 1.38 us
    reduce_scatter x3 -> x0, waiting for transfers between devices: 404 us -> none  [on_device(): lax.psum_scatter(grad.astype(wide), ('client', 'chan'), scatter_dimension...]
    all_gather x3 -> x0, waiting for transfers between devices: 179 us -> none  [on_device(): lax.all_gather(low_master[bounds[slot]:bounds[slot + 1]], ('client', 'cha...]
    pallas_call x0 -> x1, Pallas kernels: none -> 135 us  [base_pass(): pl.pallas_call(functools.partial(base_kernel, ratios), out_shape=(jax.Sha...]
    dot_general x57 -> x0, matrix products: 112 us -> none  [the longest x39 72.7 us: times_poly(): return schulz_first * left + jnp.dot(left, mixed, precision=precise)]
    psum x1 -> x0, waiting for transfers between devices: 85.8 us -> none  [schulz(): lax.psum(tuple((gram_of(section) for section in sections)), ('client', 'c...]
    pallas_call x1, Pallas kernels: 105 us -> 148 us  [client_pass(): pl.pallas_call(functools.partial(client_kernel, gather, images, classes),...]
    psum x1 -> x0, blocking collectives: 40.6 us -> none  [on_device(): lax.psum((loss_tile[0, 0], mask[0].astype(wide) * (images / halves)), ('c...]
    convert_element_type x5 -> x0, other arithmetic: 18.2 us -> none  [the longest x3 15.7 us: on_device(): grad.astype(wide)]
  transfers between devices with their start and end apart: 7 -> 0, of which waited for: 7 -> 0; matrix products, arithmetic and copies ran while one was open for 3% -> 0% of each run, Pallas kernels for 0% -> 0%
where the time goes in v3:
time: 304 us; the launch traced here: 303 us
  Pallas kernels  283 us (93%)
  local copies, waits for them, and re-layouts  16 us (5%)
    pallas_call x1, Pallas kernels, client_pass(): pl.pallas_call(functools.partial(client_kernel, gather, images, classes),...  148 us
    pallas_call x1, Pallas kernels, base_pass(): pl.pallas_call(functools.partial(base_kernel, ratios), out_shape=(jax.Sha...  135 us
    unnamed x19, local copies, waits for them, and re-layouts  12.7 us

profile of v3, /device:TPU:0, one launch (start us, length us, event | category | flops | bytes accessed | tf_op | source)
XLA Modules:
  0.0 302.8 jit_solution(14461939865289890889)
XLA Ops:
  0.6 1.2 copy.22
  1.9 0.8 pad.4.head
  2.7 1.4 copy.23.labels
  4.0 1.3 copy.49
  6.0 148.2 %shard_map.195 = (bf16[2048,512]{1,0:T(8,128)(2,1)}, bf16[4608,512]{1,0:T(8,128)(2,1)}, bf16[2048,512]{1,0:T(8,128)(2,1)}, f32[2,1536]{1,0:T(2,128)}, f32[1024,128]{1,0:T(8,128)}, /*index=5*/f32[8,128]{1,0:T(8,128)}) custom-call(bf16[3136,1024]{1,0:T(8,128)(2,1)} %bitcast.34, s32[64,1]{1,0:T(8,128)} %copy.23.labels, s32[1]{0:T(128)S(6)} %copy.53.flag, ...), custom_call_target="tpu_custom_call" | custom-call | tf_op jit(solution)/shard_map/pallas_call | solution.py:748
  154.2 0.0 copy-start
  154.2 0.0 copy-start.1
  154.2 134.9 %shard_map.196 = (f32[272,512]{1,0:T(8,128)}, f32[272,512]{1,0:T(8,128)}, bf16[272,512]{1,0:T(8,128)(2,1)}, f32[8,128]{1,0:T(8,128)}) custom-call(f32[272,512]{1,0:T(8,128)} %bitcast.37, f32[272,512]{1,0:T(8,128)} %bitcast.40, f32[272,512]{1,0:T(8,128)} %bitcast.41, f32[8,128]{1,0:T(8,128)} %get-tuple-element.20.loss_in, ...), custom_call_target="tpu_custom_call" | custom-call | tf_op jit(solution)/shard_map/pallas_call | solution.py:1213
  289.1 1.2 slice_bitcast_fusion
  290.3 0.0 copy-done
  290.3 0.4 copy.28
  290.7 0.0 copy-done.1
  290.7 0.4 copy.29
  291.1 0.0 copy-start.2
  291.1 1.5 multiply_subtract_fusion
  292.6 1.0 copy.35
  293.6 1.0 copy.36
  294.7 1.0 copy.37
  295.7 0.8 multiply_subtract_fusion.1
  296.5 0.6 copy.32
  297.1 0.6 copy.33
  297.7 0.6 copy.34
  298.3 1.9 copy.54
  300.2 1.9 copy.55
  302.1 0.0 copy-done.2
  302.1 0.7 copy.56
  (1 shorter events, 0.0 us)
Async XLA Ops:
  154.2 136.1 %copy-start = (f32[1,1024,100]{1,0,2:T(1,128)S(1)}, f32[1,1024,100]{1,0,2:T(1,128)}, u32[]{:S(2)}) copy-start(f32[1,1024,100]{1,0,2:T(1,128)} %param.22) | copy-start | bytes 1228804
  154.2 136.5 %copy-start.1 = (f32[1,1024,100]{1,0,2:T(1,128)S(1)}, f32[1,1024,100]{1,0,2:T(1,128)}, u32[]{:S(2)}) copy-start(f32[1,1024,100]{1,0,2:T(1,128)} %param.23) | copy-start | bytes 1228804
  291.1 11.0 %copy-start.2 = (bf16[272,512]{1,0:T(8,128)(2,1)S(1)}, bf16[272,512]{1,0:T(8,128)(2,1)}, u32[]{:S(2)}) copy-start(bf16[272,512]{1,0:T(8,128)(2,1)} %get-tuple-element.27) | copy-start | bytes 835588
